TPU v7x, 32 devices: a whole 2x2x4 slice. The times are simulated.
32 devices in a mesh: dp: 8 (over z, y), seq: 4 (over x, core).
Axes of the slice: x: 2, y: 2, z: 4, core: 2. Of those that a mesh axis runs over, the one named last changes fastest.
Arguments:
- tokens: float32 [8, 4096, 512], P('dp', 'seq'), may hold values from -6 to 6
- cotangent: float32 [8, 4096, 512], P('dp', 'seq'), may hold values from -6 to 6
- lengths: int32 [8, 6], P('dp'), may hold values from 1 to 4091, as said below
- routes: int32 [8, 4096, 2], P('dp', 'seq'), may hold values from 0 to 7, all different within a row
- router_weight: float32 [512, 8], P(('dp', 'seq')), may hold values from -0.1875 to 0.1875
- query_weight: float32 [512, 512], P(('dp', 'seq')), may hold values from -0.375 to 0.375
- out_weight: float32 [512, 512], P(('dp', 'seq')), may hold values from -3 to 3
- kv_weight: float32 [512, 128], P(('dp', 'seq')), may hold values from -0.375 to 0.375
- up_weight: float32 [512, 2048], P(('dp', 'seq')), may hold values from -0.25 to 0.25
- up_bias: float32 [2048], P(('dp', 'seq')), may hold values from -2 to 2
- down_weight: float32 [2048, 512], P(('dp', 'seq')), may hold values from -0.125 to 0.125
- vectors: float32 [5, 512], P(None, ('dp', 'seq'))
- router_moment: float32 [512, 8], P(('dp', 'seq')), may hold values from -2 to 2
- query_moment: float32 [512, 512], P(('dp', 'seq')), may hold values from -2 to 2
- out_moment: float32 [512, 512], P(('dp', 'seq')), may hold values from -2 to 2
- kv_moment: float32 [512, 128], P(('dp', 'seq')), may hold values from -2 to 2
- up_moment: float32 [512, 2048], P(('dp', 'seq')), may hold values from -2 to 2
- bias_moment: float32 [2048], P(('dp', 'seq')), may hold values from -2 to 2
- down_moment: float32 [2048, 512], P(('dp', 'seq')), may hold values from -2 to 2
- vector_moment: float32 [5, 512], P(None, ('dp', 'seq')), may hold values from -2 to 2
- router_average: float32 [512, 8], P(('dp', 'seq')), may hold values from -0.1875 to 0.1875
- query_average: float32 [512, 512], P(('dp', 'seq')), may hold values from -0.375 to 0.375
- out_average: float32 [512, 512], P(('dp', 'seq')), may hold values from -3 to 3
- kv_average: float32 [512, 128], P(('dp', 'seq')), may hold values from -0.375 to 0.375
- up_average: float32 [512, 2048], P(('dp', 'seq')), may hold values from -0.25 to 0.25
- bias_average: float32 [2048], P(('dp', 'seq')), may hold values from -2 to 2
- down_average: float32 [2048, 512], P(('dp', 'seq')), may hold values from -0.125 to 0.125
- vector_average: float32 [5, 512], P(None, ('dp', 'seq')), may hold values from -3 to 3
Outputs:
- output: float32 [8, 4096, 512], P('dp', 'seq')
- input_grad: float32 [8, 4096, 512], P('dp', 'seq')
- new_router: float32 [512, 8], P(('dp', 'seq'))
- new_query: float32 [512, 512], P(('dp', 'seq'))
- new_out: float32 [512, 512], P(('dp', 'seq'))
- new_kv: float32 [512, 128], P(('dp', 'seq'))
- new_up: float32 [512, 2048], P(('dp', 'seq'))
- new_bias: float32 [2048], P(('dp', 'seq'))
- new_down: float32 [2048, 512], P(('dp', 'seq'))
- new_vectors: float32 [5, 512], P(None, ('dp', 'seq'))
- new_router_moment: float32 [512, 8], P(('dp', 'seq'))
- new_query_moment: float32 [512, 512], P(('dp', 'seq'))
- new_out_moment: float32 [512, 512], P(('dp', 'seq'))
- new_kv_moment: float32 [512, 128], P(('dp', 'seq'))
- new_up_moment: float32 [512, 2048], P(('dp', 'seq'))
- new_bias_moment: float32 [2048], P(('dp', 'seq'))
- new_down_moment: float32 [2048, 512], P(('dp', 'seq'))
- new_vector_moment: float32 [5, 512], P(None, ('dp', 'seq'))
- new_router_average: float32 [512, 8], P(('dp', 'seq'))
- new_query_average: float32 [512, 512], P(('dp', 'seq'))
- new_out_average: float32 [512, 512], P(('dp', 'seq'))
- new_kv_average: float32 [512, 128], P(('dp', 'seq'))
- new_up_average: float32 [512, 2048], P(('dp', 'seq'))
- new_bias_average: float32 [2048], P(('dp', 'seq'))
- new_down_average: float32 [2048, 512], P(('dp', 'seq'))
- new_vector_average: float32 [5, 512], P(None, ('dp', 'seq'))
Inputs may be any that keep to these rules, and one draw needn't show every extreme that they name: Each row's 6 lengths sum to 4096; in every row one sentence starts among the first 1024 positions and ends among the last 1024. `routes`: the 2 experts of one token differ from each other; across the positions of a row the same experts repeat, and every expert is chosen somewhere.
All inputs are finite; a program needn't handle non-finite values.
Results may differ from a plain program's by a relative error of at most 0.0003.
Values sent between devices are 32-bit elements; how exact they have to be, the bound alone decides.
A program may use at most 320 MiB of HBM per device.

v0:
```python
import math

import jax
import jax.numpy as jnp
from jax import lax
from jax.sharding import PartitionSpec as P

highest = lax.Precision.HIGHEST
norm_eps = 1e-05
step_rate = 0.02
moment_decay = 0.9
average_decay = 0.99


def matmul(left, right):
    return jnp.dot(left, right, precision=highest, preferred_element_type=jnp.float32)


def layer_norm(values, gain, shift):
    centre = values - jnp.mean(values, axis=-1, keepdims=True)
    spread = jnp.mean(centre * centre, axis=-1, keepdims=True)
    return centre * lax.rsqrt(spread + norm_eps) * gain + shift


def project_in(row_tokens, vectors, router_weight, query_weight, kv_weight, onehot):
    normed = layer_norm(row_tokens, vectors[0], vectors[1])
    logits = matmul(normed, router_weight)
    chosen = jnp.einsum("tke,te->tk", onehot, logits, precision=highest)
    gates = jax.nn.softmax(chosen, axis=-1)
    experts = onehot.shape[2]
    all_queries = matmul(normed, query_weight).reshape(normed.shape[0], experts, -1)
    queries = jnp.einsum("tke,ted->tkd", onehot, all_queries, precision=highest)
    keyval = matmul(normed, kv_weight)
    return (queries, keyval, gates)


def project_out(
    row_tokens, heads, gates, onehot, vectors, out_weight, up_weight, up_bias, down_weight
):
    mixed = jnp.einsum("tk,tke,tkd->ted", gates, onehot, heads, precision=highest)
    mixed = mixed.reshape(row_tokens.shape[0], -1)
    middle = row_tokens + matmul(mixed, out_weight)
    normed = layer_norm(middle, vectors[2], vectors[3])
    hidden = jax.nn.gelu(matmul(normed, up_weight) + up_bias)
    return middle + matmul(hidden, down_weight) + vectors[4]


def update(weight, gradient, moment, average, factor):
    scaled = gradient * factor
    moment_new = moment_decay * moment + scaled
    weight_new = weight - step_rate * (scaled + moment_decay * moment_new)
    average_new = average_decay * average + (1.0 - average_decay) * weight_new
    return (weight_new, moment_new, average_new)


def on_device(
    tokens,
    cotangent,
    lengths,
    routes,
    router_weight,
    query_weight,
    out_weight,
    kv_weight,
    up_weight,
    up_bias,
    down_weight,
    vectors,
    router_moment,
    query_moment,
    out_moment,
    kv_moment,
    up_moment,
    bias_moment,
    down_moment,
    vector_moment,
    router_average,
    query_average,
    out_average,
    kv_average,
    up_average,
    bias_average,
    down_average,
    vector_average,
):
    full_router, full_query, full_out, full_kv, full_up, full_bias, full_down, full_vectors = (
        lax.all_gather(router_weight, ("dp", "seq"), axis=0, tiled=True),
        lax.all_gather(query_weight, ("dp", "seq"), axis=0, tiled=True),
        lax.all_gather(out_weight, ("dp", "seq"), axis=0, tiled=True),
        lax.all_gather(kv_weight, ("dp", "seq"), axis=0, tiled=True),
        lax.all_gather(up_weight, ("dp", "seq"), axis=0, tiled=True),
        lax.all_gather(up_bias, ("dp", "seq"), axis=0, tiled=True),
        lax.all_gather(down_weight, ("dp", "seq"), axis=0, tiled=True),
        lax.all_gather(vectors, ("dp", "seq"), axis=1, tiled=True),
    )
    local_tokens = tokens[0]
    local_cotangent = cotangent[0]
    span = local_tokens.shape[0]
    row_length = span * lax.axis_size("seq")
    offset = lax.axis_index("seq") * span
    ends = jnp.cumsum(lengths[0])
    positions = jnp.arange(row_length, dtype=jnp.int32)
    segment_all = jnp.sum((positions[:, None] >= ends[None, :]).astype(jnp.int32), axis=1)
    segment_local = lax.dynamic_slice_in_dim(segment_all, offset, span)
    experts = full_router.shape[1]
    onehot = (routes[0][:, :, None] == jnp.arange(experts, dtype=jnp.int32)[None, None, :]).astype(
        jnp.float32
    )

    def front(tokens_in, vectors_in, router_in, query_in, kv_in):
        return project_in(tokens_in, vectors_in, router_in, query_in, kv_in, onehot)

    (queries, keyval, gates), front_pull = jax.vjp(
        front, local_tokens, full_vectors, full_router, full_query, full_kv
    )
    head_width = queries.shape[-1]
    choices_count = queries.shape[1]
    score_scale = head_width ** (-0.5)
    kv_piece = lax.all_gather(keyval, "seq", axis=0, tiled=True)
    best = jnp.full((span, choices_count), -1e30, jnp.float32)
    keys = kv_piece[:, :head_width]
    values = kv_piece[:, head_width:]
    key_segment = segment_all
    scores = jnp.einsum("tkd,sd->tks", queries, keys, precision=highest) * score_scale
    same_sent = segment_local[:, None, None] == key_segment[None, None, :]
    peak = jnp.maximum(best, jnp.max(jnp.where(same_sent, scores, -1e30), axis=-1))
    weights_soft = jnp.where(same_sent, jnp.exp(scores - peak[..., None]), 0.0)
    total = jnp.sum(weights_soft, axis=-1)
    accum = jnp.einsum("tks,sd->tkd", weights_soft, values, precision=highest)
    best, total, accum = (peak, total, accum)
    heads = accum / total[..., None]
    logsum = best + jnp.log(total)

    def tail(tokens_in, heads_in, gates_in, vectors_in, out_in, up_in, bias_in, down_in):
        return project_out(
            tokens_in, heads_in, gates_in, onehot, vectors_in, out_in, up_in, bias_in, down_in
        )

    output, tail_pull = jax.vjp(
        tail, local_tokens, heads, gates, full_vectors, full_out, full_up, full_bias, full_down
    )
    (
        tokens_grad_tail,
        heads_grad,
        gates_grad,
        vectors_grad_tail,
        out_grad,
        up_grad,
        bias_grad,
        down_grad,
    ) = tail_pull(local_cotangent)
    row_delta = jnp.sum(heads_grad * heads, axis=-1)
    kv_piece = lax.all_gather(keyval, "seq", axis=0, tiled=True)
    keys = kv_piece[:, :head_width]
    values = kv_piece[:, head_width:]
    key_segment = segment_all
    scores = jnp.einsum("tkd,sd->tks", queries, keys, precision=highest) * score_scale
    same_sent = segment_local[:, None, None] == key_segment[None, None, :]
    weights_soft = jnp.where(same_sent, jnp.exp(scores - logsum[..., None]), 0.0)
    weights_grad = jnp.einsum("tkd,sd->tks", heads_grad, values, precision=highest)
    scores_grad = weights_soft * (weights_grad - row_delta[..., None]) * score_scale
    query_grad = jnp.einsum("tks,sd->tkd", scores_grad, keys, precision=highest)
    keys_grad = jnp.einsum("tks,tkd->sd", scores_grad, queries, precision=highest)
    values_grad = jnp.einsum("tks,tkd->sd", weights_soft, heads_grad, precision=highest)
    joined = jnp.concatenate([keys_grad, values_grad], axis=1)
    keyval_grad = joined
    query_grad, keyval_partial = (query_grad, keyval_grad)
    keyval_grad = lax.psum_scatter(keyval_partial, "seq", scatter_dimension=0, tiled=True)
    tokens_grad_front, vectors_grad_front, router_grad, query_weight_grad, kv_grad = front_pull(
        (query_grad, keyval_grad, gates_grad)
    )
    input_grad = tokens_grad_tail + tokens_grad_front
    vectors_grad = vectors_grad_tail + vectors_grad_front
    shards = (
        router_weight,
        query_weight,
        out_weight,
        kv_weight,
        up_weight,
        up_bias,
        down_weight,
        vectors,
    )
    shard_dims = (0, 0, 0, 0, 0, 0, 0, 1)
    summed = lax.psum(
        (
            router_grad,
            query_weight_grad,
            out_grad,
            kv_grad,
            up_grad,
            bias_grad,
            down_grad,
            vectors_grad,
        ),
        ("dp", "seq"),
    )
    place = lax.axis_index(("dp", "seq"))
    reduced = tuple(
        (
            lax.dynamic_slice_in_dim(
                whole_grad, place * shard.shape[shard_dim], shard.shape[shard_dim], shard_dim
            )
            for whole_grad, shard, shard_dim in zip(summed, shards, shard_dims)
        )
    )
    all_tokens = span * lax.axis_size("seq") * tokens.shape[0] * lax.axis_size("dp")
    factor = 1.0 / math.sqrt(all_tokens)
    new_router, new_router_moment, new_router_average = update(
        router_weight, reduced[0], router_moment, router_average, factor
    )
    new_query, new_query_moment, new_query_average = update(
        query_weight, reduced[1], query_moment, query_average, factor
    )
    new_out, new_out_moment, new_out_average = update(
        out_weight, reduced[2], out_moment, out_average, factor
    )
    new_kv, new_kv_moment, new_kv_average = update(
        kv_weight, reduced[3], kv_moment, kv_average, factor
    )
    new_up, new_up_moment, new_up_average = update(
        up_weight, reduced[4], up_moment, up_average, factor
    )
    new_bias, new_bias_moment, new_bias_average = update(
        up_bias, reduced[5], bias_moment, bias_average, factor
    )
    new_down, new_down_moment, new_down_average = update(
        down_weight, reduced[6], down_moment, down_average, factor
    )
    new_vectors, new_vector_moment, new_vector_average = update(
        vectors, reduced[7], vector_moment, vector_average, factor
    )
    return (
        output[None],
        input_grad[None],
        new_router,
        new_query,
        new_out,
        new_kv,
        new_up,
        new_bias,
        new_down,
        new_vectors,
        new_router_moment,
        new_query_moment,
        new_out_moment,
        new_kv_moment,
        new_up_moment,
        new_bias_moment,
        new_down_moment,
        new_vector_moment,
        new_router_average,
        new_query_average,
        new_out_average,
        new_kv_average,
        new_up_average,
        new_bias_average,
        new_down_average,
        new_vector_average,
    )


def solution(mesh):
    in_specs = (
        P("dp", "seq", None),
        P("dp", "seq", None),
        P("dp", None),
        P("dp", "seq", None),
        P(("dp", "seq"), None),
        P(("dp", "seq"), None),
        P(("dp", "seq"), None),
        P(("dp", "seq"), None),
        P(("dp", "seq"), None),
        P(("dp", "seq")),
        P(("dp", "seq"), None),
        P(None, ("dp", "seq")),
        P(("dp", "seq"), None),
        P(("dp", "seq"), None),
        P(("dp", "seq"), None),
        P(("dp", "seq"), None),
        P(("dp", "seq"), None),
        P(("dp", "seq")),
        P(("dp", "seq"), None),
        P(None, ("dp", "seq")),
        P(("dp", "seq"), None),
        P(("dp", "seq"), None),
        P(("dp", "seq"), None),
        P(("dp", "seq"), None),
        P(("dp", "seq"), None),
        P(("dp", "seq")),
        P(("dp", "seq"), None),
        P(None, ("dp", "seq")),
    )
    out_specs = (
        P("dp", "seq", None),
        P("dp", "seq", None),
        P(("dp", "seq"), None),
        P(("dp", "seq"), None),
        P(("dp", "seq"), None),
        P(("dp", "seq"), None),
        P(("dp", "seq"), None),
        P(("dp", "seq")),
        P(("dp", "seq"), None),
        P(None, ("dp", "seq")),
        P(("dp", "seq"), None),
        P(("dp", "seq"), None),
        P(("dp", "seq"), None),
        P(("dp", "seq"), None),
        P(("dp", "seq"), None),
        P(("dp", "seq")),
        P(("dp", "seq"), None),
        P(None, ("dp", "seq")),
        P(("dp", "seq"), None),
        P(("dp", "seq"), None),
        P(("dp", "seq"), None),
        P(("dp", "seq"), None),
        P(("dp", "seq"), None),
        P(("dp", "seq")),
        P(("dp", "seq"), None),
        P(None, ("dp", "seq")),
    )
    return jax.shard_map(
        on_device, mesh=mesh, in_specs=in_specs, out_specs=out_specs, check_vma=False
    )
```

profile of v0, /device:TPU:0, one launch (start us, length us, event | category | flops | bytes accessed | tf_op | source)
XLA Modules:
  0.0 875.7 jit_solution(5250262368686756903)
XLA Ops:
  8.0 1.9 copy.132
  9.9 1.8 reduce_sum.167
  11.8 43.6 %all-gather = f32[32,16,5]{1,2,0:T(8,128)S(1)} all-gather(f32[1,16,5]{1,2,0:T(8,128)S(1)} %bitcast.173), channel_id=1, replica_groups=mesh['dp'=8,'seq'=4] {'dp','seq'}, dimensions={0}, use_global_device_ids=true | all-gather | bytes 10560 | tf_op jit(solution)/shard_map/all_gather | solution.py:94
  55.5 37.4 %all_gather.31 = f32[512,128]{1,0:T(8,128)S(1)} all-gather(f32[16,128]{1,0:T(8,128)S(1)} %copy-done.56), channel_id=1, replica_groups=mesh['dp'=8,'seq'=4] {'dp','seq'}, dimensions={0}, use_global_device_ids=true | all-gather | bytes 270336 | tf_op jit(solution)/shard_map/all_gather | solution.py:90
  93.8 4.4 fusion.91
  100.2 38.8 %all-gather.1 = f32[32,16,8]{1,2,0:T(8,128)S(1)} all-gather(f32[1,16,8]{1,2,0:T(8,128)S(1)} %bitcast.172), channel_id=1, replica_groups=mesh['dp'=8,'seq'=4] {'dp','seq'}, dimensions={0}, use_global_device_ids=true | all-gather | bytes 16896 | tf_op jit(solution)/shard_map/all_gather | solution.py:87
  139.4 3.6 fusion.92
  143.0 5.8 fusion.58
  150.1 1.1 fusion.69
  151.2 2.4 reduce_sum.190
  153.6 2.9 copy.144
  157.0 37.2 %all-reduce.5 = f32[2048]{0:T(1024)S(1)} all-reduce(f32[2048]{0:T(1024)S(1)} %dynamic-update-slice), channel_id=1, replica_groups=mesh['dp'=8,'seq'=4] {'dp','seq'}, use_global_device_ids=true, to_apply=%add.5 | all-reduce | flops 2048 | bytes 16384
  194.3 4.8 broadcast_compare_fusion
  199.1 1.6 copy.136
  200.7 6.8 fusion.23
  207.5 3.9 copy.137
  211.4 6.3 fusion.57
  217.8 1.4 copy.138
  219.2 38.7 %select_reduce_fusion = (f32[1024,2]{0,1:T(2,128)S(1)}, f32[1024,2,4096]{2,0,1:T(8,128)}) fusion(pred[1024,4096]{1,0:T(8,128)(4,1)} %broadcast_compare_fusion, f32[1024,2,64]{0,2,1:T(8,128)S(1)} %copy.138, f32[4096,128]{1,0:T(8,128)} %all-gather.10.cloned.1.call-done), kind=kOutput, calls=%fused_computation.3 | convolution fusion | flops 6467614720 | bytes 40378368 | tf_op jit(solution)/shard_map/tkd,sd->tks/dot_general | solution.py:124
  258.0 15.6 %fusion = f32[1024,2]{0,1:T(2,128)S(1)} fusion(f32[1024,2,4096]{2,0,1:T(8,128)} %get-tuple-element.174, f32[1024,2]{0,1:T(2,128)S(1)} %broadcast_maximum_fusion, pred[1024,4096]{1,0:T(8,128)(4,1)S(1)} %copy-done.7), kind=kLoop, calls=%fused_computation.4 | loop fusion | flops 33552384 | bytes 37765120 | tf_op jit(solution)/shard_map/reduce_sum | solution.py:128
  273.7 43.5 %fusion.34 = f32[1024,2,64]{0,2,1:T(8,128)S(1)} fusion(f32[4096,128]{1,0:T(8,128)S(1)} %copy-done.20, f32[1024,2,4096]{2,0,1:T(8,128)} %get-tuple-element.174, f32[1024,2]{0,1:T(2,128)S(1)} %broadcast_maximum_fusion, pred[1024,4096]{1,0:T(8,128)(4,1)S(1)} %copy-done.7, f32[1024,2]{0,1:T(2,128)S(1)} %fusion), kind=kOutput, calls=%fused_computation.64 | convolution fusion | flops 6467747840 | bytes 40386560 | tf_op jit(solution)/shard_map/tks,sd->tkd/dot_general | solution.py:129
  317.2 1.3 copy.141
  318.4 13.4 %fusion.37 = f32[1024,8,64]{2,1,0:T(8,128)} fusion(f32[1024,2,64]{2,1,0:T(2,128)} %copy.141, f32[1024,2]{1,0:T(8,128)} %fusion.69, s32[1024,2]{1,0:T(8,128)S(1)} %copy-done.27), kind=kOutput, calls=%fused_computation.67 | convolution fusion | flops 12615680 | bytes 2637824 | tf_op jit(solution)/shard_map/jvp(tk,tke,tkd->ted)/dot_general | solution.py:40
  331.8 3.8 copy.142
  335.6 5.5 fusion.95
  341.1 1.3 copy-done
  342.8 18.4 %fusion.30 = f32[1024,2048]{1,0:T(8,128)} fusion(f32[512,2048]{1,0:T(8,128)} %all-gather.14.cloned.1.call-done, f32[1024,512]{0,1:T(8,128)} %copy-done, f32[512]{0:T(512)S(1)} %bitcast.180, f32[512]{0:T(512)S(1)} %bitcast.167, f32[1024]{0:T(1024)S(1)} %fusion.72, f32[1024]{0:T(1024)S(1)} %broadcast_multiply_fusion), kind=kOutput, calls=%fused_computation.59 | convolution fusion | flops 12886999040 | bytes 14692352 | tf_op jit(solution)/shard_map/jvp()/dot_general | solution.py:16
  361.1 21.8 %fusion.96 = (f32[2048]{0:T(1024)S(1)}, f32[1024,2048]{1,0:T(8,128)S(1)}) fusion(f32[1024,2048]{1,0:T(8,128)} %fusion.30, f32[2048]{0:T(1024)S(1)} %all-reduce.5, f32[2048,512]{1,0:T(8,128)} %all-gather.16.cloned.1.call-done, f32[1,1024,512]{2,1,0:T(8,128)} %param.29), kind=kOutput, calls=%fused_computation.177 | convolution fusion | flops 12928940032 | bytes 23085056 | tf_op jit(solution)/shard_map/transpose(jvp())/dot_general | solution.py:16
  382.9 15.3 %fusion.97 = (f32[512]{0:T(512)S(1)}, f32[1024,512]{1,0:T(8,128)}) fusion(f32[1024,2048]{1,0:T(8,128)S(1)} %get-tuple-element.179, f32[512,2048]{1,0:T(8,128)S(1)} %copy-done.76), kind=kOutput, calls=%fused_computation.178 | convolution fusion | flops 12885426176 | bytes 14682112 | tf_op jit(solution)/shard_map/transpose(jvp())/dot_general | solution.py:16
  398.2 3.1 copy.145
  401.3 2.7 multiply_reduce_fusion.3
  407.6 4.8 fusion.98
  412.4 3.9 copy.146
  416.3 10.4 %fusion.35 = f32[1024,2,64]{2,1,0:T(2,128)} fusion(f32[1024,8,64]{2,1,0:T(8,128)} %copy.146, f32[1024,2]{1,0:T(8,128)} %fusion.69, s32[1024,2]{1,0:T(8,128)S(1)} %copy-done.27), kind=kOutput, calls=%fused_computation.65 | convolution fusion | flops 12615680 | bytes 2637824 | tf_op jit(solution)/shard_map/transpose(jvp(tk,tke,tkd->ted))/dot_general | solution.py:40
  426.7 1.4 copy.147
  428.2 33.3 %fusion.17 = f32[4096,64]{0,1:T(8,128)} fusion(f32[1024,2,64]{0,2,1:T(8,128)S(1)} %copy.147, f32[1024,2,4096]{2,0,1:T(8,128)} %get-tuple-element.174, f32[1024,2]{0,1:T(2,128)S(1)} %log_add_fusion, pred[1024,4096]{1,0:T(8,128)(4,1)} %broadcast_compare_fusion), kind=kOutput, calls=%fused_computation.25 | convolution fusion | flops 6467616768 | bytes 39329792 | tf_op jit(solution)/shard_map/tks,tkd->sd/dot_general | solution.py:164
  461.6 47.0 %multiply_multiply_fusion = f32[1024,2,4096]{2,0,1:T(8,128)} fusion(f32[1024,2,4096]{2,0,1:T(8,128)} %get-tuple-element.174, f32[1024,2]{0,1:T(2,128)S(1)} %multiply_reduce_fusion.7, f32[1024,2]{0,1:T(2,128)S(1)} %log_add_fusion, pred[1024,4096]{1,0:T(8,128)(4,1)S(1)} %copy-done.8, f32[1024,2,64]{0,2,1:T(8,128)S(1)} %copy.147, f32[4096,128]{1,0:T(8,128)S(1)} %copy-done.21), kind=kOutput, calls=%fused_computation | convolution fusion | flops 6492782592 | bytes 73940992 | tf_op jit(solution)/shard_map/tkd,sd->tks/dot_general | solution.py:160
  508.5 25.3 %convolution_bitcast_fusion = f32[4096,64]{0,1:T(8,128)S(1)} fusion(f32[1024,2,4096]{2,0,1:T(8,128)} %multiply_multiply_fusion, f32[1024,2,64]{0,2,1:T(8,128)} %copy-done.19), kind=kOutput, calls=%fused_computation.26 | convolution fusion | flops 6442450944 | bytes 35127296 | tf_op jit(solution)/shard_map/tks,tkd->sd/dot_general | solution.py:163
  533.8 2.8 pad_maximum_fusion
  536.7 37.2 %fusion.27 = f32[1024,2,64]{0,2,1:T(8,128)S(1)} fusion(f32[1024,2,4096]{2,0,1:T(8,128)} %multiply_multiply_fusion, f32[4096,128]{1,0:T(8,128)} %all-gather.10.cloned.1.call-done), kind=kOutput, calls=%fused_computation.56 | convolution fusion | flops 6442450944 | bytes 36175872 | tf_op jit(solution)/shard_map/tks,sd->tkd/dot_general | solution.py:162
  573.9 1.3 copy.153
  575.2 7.9 fusion.56
  583.1 4.2 copy.154
  587.4 6.9 fusion.101
  594.4 8.1 fusion.25
  602.5 18.2 %fusion.29 = f32[512,2048]{1,0:T(8,128)} fusion(f32[1024,2048]{1,0:T(8,128)} %copy-done.78, f32[1024,512]{0,1:T(8,128)S(1)} %copy-done.2, f32[512]{0:T(512)S(1)} %bitcast.181, f32[512]{0:T(512)S(1)} %bitcast.171, f32[1024]{0:T(1024)S(1)} %fusion.72, f32[1024]{0:T(1024)S(1)} %broadcast_multiply_fusion), kind=kOutput, calls=%fused_computation.58 | convolution fusion | flops 12886999040 | bytes 14692352 | tf_op jit(solution)/shard_map/transpose(jvp())/dot_general | solution.py:16
  620.7 17.1 %fusion.18 = f32[2048,512]{1,0:T(8,128)} fusion(f32[1024,2048]{1,0:T(8,128)S(1)} %bitcast.187, f32[2048]{0:T(1024)S(1)} %all-reduce.5, f32[1,1024,512]{2,1,0:T(8,128)S(1)} %copy-done.14), kind=kOutput, calls=%fused_computation.29 | convolution fusion | flops 12903776256 | bytes 14688256 | tf_op jit(solution)/shard_map/transpose(jvp())/dot_general | solution.py:16
  637.8 3.7 fusion.89
  642.2 21.2 %add_bitcast_fusion.1 = f32[1,1024,512]{1,2,0:T(8,128)} fusion(f32[1024,512]{0,1:T(8,128)} %copy-done, f32[2048,512]{1,0:T(8,128)} %all-gather.16.cloned.1.call-done, f32[1024,2048]{1,0:T(8,128)} %fusion.30, f32[2048]{0:T(1024)S(1)} %all-reduce.5, f32[512]{0:T(512)S(1)} %bitcast.179), kind=kOutput, calls=%fused_computation.50 | convolution fusion | flops 12904824832 | bytes 16787456 | tf_op jit(solution)/shard_map/jvp()/dot_general | solution.py:16
  663.4 3.0 copy.161
  666.4 16.7 %fusion.33 = f32[1024,2]{1,0:T(8,128)S(1)} fusion(f32[1024,2,64]{2,1,0:T(2,128)S(1)} %copy-done.23, f32[1024,8,64]{2,1,0:T(8,128)} %copy.146, s32[1024,2]{1,0:T(8,128)} %copy-done.26), kind=kOutput, calls=%fused_computation.63 | convolution fusion | flops 12630016 | bytes 2637824 | tf_op jit(solution)/shard_map/transpose(jvp(tk,tke,tkd->ted))/dot_general | solution.py:40
  684.2 5.9 fusion.55
  690.1 1.8 fusion.100
  692.0 2.2 fusion.90
  694.3 3.6 fusion.99
  697.9 2.5 fusion.93
  702.0 2.0 add_bitcast_fusion
  704.3 3.2 copy.162
  707.5 42.6 %all-reduce.6 = (f32[512,8]{0,1:T(8,128)S(1)}, f32[2048]{0:T(1024)S(1)}, f32[5,512]{1,0:T(8,128)S(1)}) all-reduce(f32[512,8]{0,1:T(8,128)S(1)} %fusion.90, f32[2048]{0:T(1024)S(1)} %get-tuple-element.178, f32[5,512]{1,0:T(8,128)S(1)} %add_add_fusion.3), channel_id=1, replica_groups=mesh['dp'=8,'seq'=4] {'dp','seq'}, use_global_device_ids=true, to_apply=%region_17.18 | all-reduce | flops 8704 | bytes 69632 | tf_op jit(solution)/shard_map/psum | solution.py:185
  752.1 110.3 %all-reduce.10.cloned.1.call-done = (f32[512,512]{1,0:T(8,128)}, f32[512,512]{1,0:T(8,128)}, f32[512,128]{1,0:T(8,128)}, f32[512,2048]{1,0:T(8,128)}, f32[2048,512]{1,0:T(8,128)}) async-done(((f32[512,512]{1,0:T(8,128)}, f32[512,512]{1,0:T(8,128)}, f32[512,128]{1,0:T(8,128)}, f32[512,2048]{1,0:T(8,128)}, f32[2048,512]{1,0:T(8,128)}), (f32[512,512]{1,0:T(8,128)}, f32[512,512]{1,0:T(8,128)}, ...) | async-done | bytes 10747920 | tf_op jit(solution)/shard_map/psum | solution.py:185
  862.4 1.7 multiply_add_fusion.7
  864.1 1.3 multiply_add_fusion.15
  865.5 1.7 multiply_add_fusion.8
  867.2 1.5 multiply_add_fusion.11
  (219 shorter events, 15.5 us)
Async XLA Ops:
  7.2 191.9 %all-gather.8.cloned.1.call-start = ((), (), s32[]{:S(2)}) async-start(), calls=%async_computation.1 | async-start | bytes 1081344 | tf_op jit(solution)/shard_map/all_gather | solution.py:88
  7.9 211.3 %all-gather.10.cloned.1.call-start = ((), (), s32[]{:S(2)}) async-start(), calls=%async_computation.2 | async-start | bytes 2621440 | tf_op jit(solution)/shard_map/all_gather | solution.py:119
  9.9 45.6 %copy-start.56 = (f32[16,128]{1,0:T(8,128)S(1)}, f32[16,128]{1,0:T(8,128)}, u32[]{:S(2)}) copy-start(f32[16,128]{1,0:T(8,128)} %param.35) | copy-start | bytes 24580
  92.9 107.8 %copy-start.30 = (f32[1024]{0:T(1024)}, f32[1024]{0:T(1024)S(1)}, u32[]{:S(2)}) copy-start(f32[1024]{0:T(1024)S(1)} %broadcast_multiply_fusion.1) | copy-start | bytes 12292
  93.2 7.0 copy-start.50
  93.2 7.0 copy-start.59
  93.2 107.4 %copy-start.32 = (f32[1024]{0:T(1024)}, f32[1024]{0:T(1024)S(1)}, u32[]{:S(2)}) copy-start(f32[1024]{0:T(1024)S(1)} %fusion.71) | copy-start | bytes 12292
  93.8 106.9 %copy-start.34 = (f32[1,512]{1,0:T(1,128)}, f32[1,512]{1,0:T(1,128)S(1)}, u32[]{:S(2)}) copy-start(f32[1,512]{1,0:T(1,128)S(1)} %get-tuple-element.172) | copy-start | bytes 6148
  93.8 106.9 %copy-start.48 = (f32[1,512]{1,0:T(1,128)}, f32[1,512]{1,0:T(1,128)S(1)}, u32[]{:S(2)}) copy-start(f32[1,512]{1,0:T(1,128)S(1)} %get-tuple-element.171) | copy-start | bytes 6148
  93.8 45.3 %copy-start.63 = (s32[1,1024,2]{1,2,0:T(2,128)S(1)}, s32[1,1024,2]{1,2,0:T(2,128)}, u32[]{:S(2)}) copy-start(s32[1,1024,2]{1,2,0:T(2,128)} %param.31) | copy-start | bytes 24580
  98.3 237.4 %all-gather.12.cloned.1.call-start = ((), (), s32[]{:S(2)}) async-start(), calls=%async_computation.3 | async-start | bytes 1081344 | tf_op jit(solution)/shard_map/all_gather | solution.py:89
  99.0 243.8 %all-gather.14.cloned.1.call-start = ((), (), s32[]{:S(2)}) async-start(), calls=%async_computation.4 | async-start | bytes 4325376 | tf_op jit(solution)/shard_map/all_gather | solution.py:91
  99.6 261.6 %all-gather.16.cloned.1.call-start = ((), (), s32[]{:S(2)}) async-start(), calls=%async_computation.5 | async-start | bytes 4325376 | tf_op jit(solution)/shard_map/all_gather | solution.py:93
  100.2 537.6 %reduce-scatter.2.cloned.1.call-start = ((), (), s32[]{:S(2)}) async-start(), calls=%async_computation.6 | async-start | bytes 2621440 | tf_op jit(solution)/shard_map/reduce_scatter | solution.py:168
  139.4 9.4 %copy-start.26 = (s32[1024,2]{1,0:T(8,128)}, s32[1024,2]{1,0:T(8,128)S(1)}, u32[]{:S(2)}) copy-start(s32[1024,2]{1,0:T(8,128)S(1)} %copy.133) | copy-start | bytes 24580
  149.1 7.4 copy-start.42
  149.5 7.1 copy-start.44
  219.2 38.8 %copy-start.19 = (f32[1024,2,64]{0,2,1:T(8,128)}, f32[1024,2,64]{0,2,1:T(8,128)S(1)}, u32[]{:S(2)}) copy-start(f32[1024,2,64]{0,2,1:T(8,128)S(1)} %copy.138) | copy-start | bytes 1572868
  219.2 38.8 %copy-start.7 = (pred[1024,4096]{1,0:T(8,128)(4,1)S(1)}, pred[1024,4096]{1,0:T(8,128)(4,1)}, u32[]{:S(2)}) copy-start(pred[1024,4096]{1,0:T(8,128)(4,1)} %broadcast_compare_fusion) | copy-start | bytes 12582916
  258.0 15.7 %copy-start.20 = (f32[4096,128]{1,0:T(8,128)S(1)}, f32[4096,128]{1,0:T(8,128)}, u32[]{:S(2)}) copy-start(f32[4096,128]{1,0:T(8,128)} %all-gather.10.cloned.1.call-done) | copy-start | bytes 6291460
  361.1 21.8 %copy-start.76 = (f32[512,2048]{1,0:T(8,128)S(1)}, f32[512,2048]{1,0:T(8,128)}, u32[]{:S(2)}) copy-start(f32[512,2048]{1,0:T(8,128)} %all-gather.14.cloned.1.call-done) | copy-start | bytes 12582916
  382.9 15.3 %copy-start.78 = (f32[1024,2048]{1,0:T(8,128)}, f32[1024,2048]{1,0:T(8,128)S(1)}, u32[]{:S(2)}) copy-start(f32[1024,2048]{1,0:T(8,128)S(1)} %get-tuple-element.179) | copy-start | bytes 25165828
  428.2 33.3 %copy-start.8 = (pred[1024,4096]{1,0:T(8,128)(4,1)S(1)}, pred[1024,4096]{1,0:T(8,128)(4,1)}, u32[]{:S(2)}) copy-start(pred[1024,4096]{1,0:T(8,128)(4,1)} %broadcast_compare_fusion) | copy-start | bytes 12582916
  428.2 33.3 %copy-start.21 = (f32[4096,128]{1,0:T(8,128)S(1)}, f32[4096,128]{1,0:T(8,128)}, u32[]{:S(2)}) copy-start(f32[4096,128]{1,0:T(8,128)} %all-gather.10.cloned.1.call-done) | copy-start | bytes 6291460
  536.6 38.6 %copy-start.28 = (s32[1024,2]{1,0:T(8,128)S(1)}, s32[1024,2]{1,0:T(8,128)}, u32[]{:S(2)}) copy-start(s32[1024,2]{1,0:T(8,128)} %copy-done.26) | copy-start | bytes 24580
  536.6 325.8 %all-reduce.10.cloned.1.call-start = ((), (), s32[]{:S(2)}) async-start(), calls=%async_computation.7 | async-start | bytes 21495808 | tf_op jit(solution)/shard_map/psum | solution.py:185
  587.3 7.0 copy-start.6
  587.3 7.0 copy-start.12
  587.3 7.0 copy-start.31
  587.4 7.0 copy-start.33
  587.4 7.0 copy-start.35
  587.4 7.0 copy-start.49
  594.4 8.1 copy-start.2
  594.4 26.3 %slice-start = ((s8[8388608]{0:T(1024)(128)(4,1)}), s8[4194304]{0:T(1024)(128)(4,1)S(1)}, s32[]{:S(2)}) async-start(s8[8388608]{0:T(1024)(128)(4,1)} %bitcast.186), calls=%async_computation.8 | async-start | bytes 8388608
  602.5 18.2 %copy-start.14 = (f32[1,1024,512]{2,1,0:T(8,128)S(1)}, f32[1,1024,512]{2,1,0:T(8,128)}, u32[]{:S(2)}) copy-start(f32[1,1024,512]{2,1,0:T(8,128)} %param.29) | copy-start | bytes 6291460
  602.5 18.2 %slice-start.1 = ((s8[8388608]{0:T(1024)(128)(4,1)}), s8[4194304]{0:T(1024)(128)(4,1)S(1)}, s32[]{:S(2)}) async-start(s8[8388608]{0:T(1024)(128)(4,1)} %bitcast.186), calls=%async_computation.9 | async-start | bytes 8388608
  666.4 16.7 %copy-start.10 = (f32[1024,1,2]{2,1,0:T(1,128)S(1)}, f32[1024,1,2]{2,1,0:T(1,128)}, u32[]{:S(2)}) copy-start(f32[1024,1,2]{2,1,0:T(1,128)} %copy-done.9) | copy-start | bytes 24580
  666.4 16.7 %copy-start.43 = (f32[1024]{0:T(1024)S(1)}, f32[1024]{0:T(1024)}, u32[]{:S(2)}) copy-start(f32[1024]{0:T(1024)} %copy-done.42) | copy-start | bytes 12292
  666.4 16.7 %copy-start.58 = (f32[1024]{0:T(1024)S(1)}, f32[1024]{0:T(1024)}, u32[]{:S(2)}) copy-start(f32[1024]{0:T(1024)} %multiply_divide_fusion) | copy-start | bytes 12292
  666.4 17.2 %copy-start.45 = (f32[1024]{0:T(1024)S(1)}, f32[1024]{0:T(1024)}, u32[]{:S(2)}) copy-start(f32[1024]{0:T(1024)} %copy-done.44) | copy-start | bytes 12292
  704.0 46.1 %copy-start.73 = (f32[64]{0:T(128)S(1)}, f32[64]{0:T(128)}, u32[]{:S(2)}) copy-start(f32[64]{0:T(128)} %param.37) | copy-start | bytes 772
  704.0 46.1 %copy-start.74 = (f32[64]{0:T(128)S(1)}, f32[64]{0:T(128)}, u32[]{:S(2)}) copy-start(f32[64]{0:T(128)} %param.53) | copy-start | bytes 772
  704.0 46.1 %copy-start.75 = (f32[64]{0:T(128)S(1)}, f32[64]{0:T(128)}, u32[]{:S(2)}) copy-start(f32[64]{0:T(128)} %param.45) | copy-start | bytes 772
  704.0 46.7 %copy-start.60 = (f32[16,8]{0,1:T(8,128)S(1)}, f32[16,8]{0,1:T(8,128)}, u32[]{:S(2)}) copy-start(f32[16,8]{0,1:T(8,128)} %param.32) | copy-start | bytes 1540
  704.0 46.7 %copy-start.67 = (f32[16,8]{0,1:T(8,128)S(1)}, f32[16,8]{0,1:T(8,128)}, u32[]{:S(2)}) copy-start(f32[16,8]{0,1:T(8,128)} %param.48) | copy-start | bytes 1540
  704.0 46.7 %copy-start.68 = (f32[16,8]{0,1:T(8,128)S(1)}, f32[16,8]{0,1:T(8,128)}, u32[]{:S(2)}) copy-start(f32[16,8]{0,1:T(8,128)} %param.40) | copy-start | bytes 1540
  704.0 47.4 %copy-start.62 = (f32[5,16]{1,0:T(8,128)S(1)}, f32[5,16]{1,0:T(8,128)}, u32[]{:S(2)}) copy-start(f32[5,16]{1,0:T(8,128)} %param.39) | copy-start | bytes 964
  704.1 47.4 %copy-start.69 = (f32[5,16]{1,0:T(8,128)S(1)}, f32[5,16]{1,0:T(8,128)}, u32[]{:S(2)}) copy-start(f32[5,16]{1,0:T(8,128)} %param.55) | copy-start | bytes 964
  704.1 47.4 %copy-start.70 = (f32[5,16]{1,0:T(8,128)S(1)}, f32[5,16]{1,0:T(8,128)}, u32[]{:S(2)}) copy-start(f32[5,16]{1,0:T(8,128)} %param.47) | copy-start | bytes 964
  704.1 158.3 %copy-start.24 = (f32[64,512]{1,0:T(8,128)S(1)}, f32[64,512]{1,0:T(8,128)}, u32[]{:S(2)}) copy-start(f32[64,512]{1,0:T(8,128)} %param.38) | copy-start | bytes 393220
  704.1 158.3 %copy-start.36 = (f32[64,512]{1,0:T(8,128)S(1)}, f32[64,512]{1,0:T(8,128)}, u32[]{:S(2)}) copy-start(f32[64,512]{1,0:T(8,128)} %param.54) | copy-start | bytes 393220
  704.1 158.3 %copy-start.37 = (f32[64,512]{1,0:T(8,128)S(1)}, f32[64,512]{1,0:T(8,128)}, u32[]{:S(2)}) copy-start(f32[64,512]{1,0:T(8,128)} %param.46) | copy-start | bytes 393220
  704.1 160.0 %copy-start.57 = (f32[16,128]{1,0:T(8,128)S(1)}, f32[16,128]{1,0:T(8,128)}, u32[]{:S(2)}) copy-start(f32[16,128]{1,0:T(8,128)} %param.35) | copy-start | bytes 24580
  704.1 160.0 %copy-start.64 = (f32[16,128]{1,0:T(8,128)S(1)}, f32[16,128]{1,0:T(8,128)}, u32[]{:S(2)}) copy-start(f32[16,128]{1,0:T(8,128)} %param.51) | copy-start | bytes 24580
  704.1 160.0 %copy-start.65 = (f32[16,128]{1,0:T(8,128)S(1)}, f32[16,128]{1,0:T(8,128)}, u32[]{:S(2)}) copy-start(f32[16,128]{1,0:T(8,128)} %param.43) | copy-start | bytes 24580
  704.2 161.3 %copy-start.25 = (f32[16,2048]{1,0:T(8,128)S(1)}, f32[16,2048]{1,0:T(8,128)}, u32[]{:S(2)}) copy-start(f32[16,2048]{1,0:T(8,128)} %param.36) | copy-start | bytes 393220
  704.2 161.3 %copy-start.38 = (f32[16,2048]{1,0:T(8,128)S(1)}, f32[16,2048]{1,0:T(8,128)}, u32[]{:S(2)}) copy-start(f32[16,2048]{1,0:T(8,128)} %param.52) | copy-start | bytes 393220
  704.2 161.3 %copy-start.39 = (f32[16,2048]{1,0:T(8,128)S(1)}, f32[16,2048]{1,0:T(8,128)}, u32[]{:S(2)}) copy-start(f32[16,2048]{1,0:T(8,128)} %param.44) | copy-start | bytes 393220
  704.2 163.0 %copy-start.40 = (f32[16,512]{1,0:T(8,128)S(1)}, f32[16,512]{1,0:T(8,128)}, u32[]{:S(2)}) copy-start(f32[16,512]{1,0:T(8,128)} %param.33) | copy-start | bytes 98308
  704.2 163.0 %copy-start.41 = (f32[16,512]{1,0:T(8,128)S(1)}, f32[16,512]{1,0:T(8,128)}, u32[]{:S(2)}) copy-start(f32[16,512]{1,0:T(8,128)} %param.34) | copy-start | bytes 98308
  704.2 162.9 %copy-start.52 = (f32[16,512]{1,0:T(8,128)S(1)}, f32[16,512]{1,0:T(8,128)}, u32[]{:S(2)}) copy-start(f32[16,512]{1,0:T(8,128)} %param.50) | copy-start | bytes 98308
  704.2 162.9 %copy-start.53 = (f32[16,512]{1,0:T(8,128)S(1)}, f32[16,512]{1,0:T(8,128)}, u32[]{:S(2)}) copy-start(f32[16,512]{1,0:T(8,128)} %param.42) | copy-start | bytes 98308
  704.2 162.9 %copy-start.54 = (f32[16,512]{1,0:T(8,128)S(1)}, f32[16,512]{1,0:T(8,128)}, u32[]{:S(2)}) copy-start(f32[16,512]{1,0:T(8,128)} %param.41) | copy-start | bytes 98308
  704.2 162.9 %copy-start.55 = (f32[16,512]{1,0:T(8,128)S(1)}, f32[16,512]{1,0:T(8,128)}, u32[]{:S(2)}) copy-start(f32[16,512]{1,0:T(8,128)} %param.49) | copy-start | bytes 98308
  (24 other events, 70.4 us)
Sparse Core Ops, SparseCore 0:
  10.9 56.7 all-gather.7
  98.4 20.6 all-gather.9
  122.0 53.7 all-gather.11
  178.4 61.1 all-gather.13
  242.4 60.6 all-gather.15
  536.7 31.9 reduce-scatter.1
  641.6 220.7 all-reduce.9
where the time goes:
time: 881 us; the launch traced here: 876 us
  matrix products  457 us (52%)
  blocking collectives  200 us (23%)
  waiting for transfers between devices  113 us (13%)
  other arithmetic  46.9 us (5%)
  local copies, waits for them, and re-layouts  43.5 us (5%)
  between operations  15.4 us (2%)
    dot_general x18, matrix products, matmul(): jnp.dot(left, right, precision=highest, preferred_element_type=jnp.float32)  166 us
    psum x1, waiting for transfers between devices, on_device(): lax.psum((router_grad, query_weight_grad, out_grad, kv_grad, up_grad, bia...  110 us
    dot_general x1, matrix products, on_device(): jnp.einsum('tkd,sd->tks', heads_grad, values, precision=highest)  47 us
    all_gather x1, blocking collectives, on_device(): lax.all_gather(vectors, ('dp', 'seq'), axis=1, tiled=True)  43.6 us
    dot_general x1, matrix products, on_device(): accum = jnp.einsum('tks,sd->tkd', weights_soft, values, precision=highest)  43.5 us
    psum x1, blocking collectives, on_device(): lax.psum((router_grad, query_weight_grad, out_grad, kv_grad, up_grad, bia...  42.6 us
    dot_general x3, matrix products, project_out(): jnp.einsum('tk,tke,tkd->ted', gates, onehot, heads, precision=highest)  40.5 us
    all_gather x1, blocking collectives, on_device(): lax.all_gather(router_weight, ('dp', 'seq'), axis=0, tiled=True)  38.8 us
  transfers between devices with their start and end apart: 7, of which 1 were waited for; matrix products, arithmetic and copies ran while one was open for 41% of the time, Pallas kernels for 0%

commit v1 on v0

--- a/solution.py
+++ b/solution.py
@@ -1,8 +1,11 @@
+import functools
 import math
 
 import jax
 import jax.numpy as jnp
 from jax import lax
+from jax.experimental import pallas as pl
+from jax.experimental.pallas import tpu as pltpu
 from jax.sharding import PartitionSpec as P
 
 highest = lax.Precision.HIGHEST
@@ -53,7 +56,7 @@
     return (weight_new, moment_new, average_new)
 
 
-def on_device(
+def general_step(
     tokens,
     cotangent,
     lengths,
@@ -260,6 +263,1019 @@
     )
 
 
+f32 = jnp.float32
+bf16 = jnp.bfloat16
+MESH = pl.DeviceIdType.MESH
+log2e = math.log2(math.e)
+far = 2.0**100
+vmem_limit = 60 * 2**20
+NN = (((1,), (0,)), ((), ()))
+NT = (((1,), (1,)), ((), ()))
+TN = (((0,), (0,)), ((), ()))
+
+
+def dot(left, right, dims=NN):
+    return lax.dot_general(left, right, dims, preferred_element_type=f32)
+
+
+def split(values):
+    high = values.astype(bf16)
+    return high, (values - high.astype(f32)).astype(bf16)
+
+
+def split_wide(values):
+    high = values.astype(bf16).astype(f32)
+    return high, values - high
+
+
+def cat(parts, axis):
+    return jnp.concatenate(parts, axis=axis)
+
+
+def dot_nn(left, right):
+    return dot(cat([left[0], left[1], left[0]], 1), cat([right[0], right[0], right[1]], 0))
+
+
+def dot_nt(left, right):
+    return dot(cat([left[0], left[1], left[0]], 1), cat([right[0], right[0], right[1]], 1), NT)
+
+
+def dot_tn(left, right):
+    return dot(cat([left[0], left[1], left[0]], 0), cat([right[0], right[0], right[1]], 0), TN)
+
+
+def iota(shape, dim):
+    return lax.broadcasted_iota(jnp.int32, shape, dim)
+
+
+def rows_at(index, count):
+    return pl.ds(pl.multiple_of(index * count, count), count)
+
+
+class Grid:
+    def __init__(self, mesh):
+        dp, seq = mesh.shape["dp"], mesh.shape["seq"]
+        self.x = max(seq // 2, 1)
+        self.y = self.x if dp % self.x == 0 else 1
+        self.z = dp // self.y
+        self.count = dp * seq
+        self.lead = (self.z, self.y, self.x, 2)
+
+    def here(self):
+        dp, seq = lax.axis_index("dp"), lax.axis_index("seq")
+        return dp // self.y, dp % self.y, seq // 2, seq % 2
+
+    def device(self, z, y, x, core):
+        return (z * self.y + y, x * 2 + core)
+
+    def others(self, axis):
+        z, y, x, core = self.here()
+        if axis == "z":
+            return [self.device((z + i) % self.z, y, x, core) for i in range(1, self.z)]
+        if axis == "y":
+            return [self.device(z, (y + i) % self.y, x, core) for i in range(1, self.y)]
+        if axis == "x":
+            return [self.device(z, y, (x + i) % self.x, core) for i in range(1, self.x)]
+        return [self.device(z, y, x, 1 - core)]
+
+    def copies(self):
+        return self.z + self.y + self.x - 2
+
+    def barrier(self):
+        barrier = pltpu.get_barrier_semaphore()
+        count = 0
+        for axis in "zyxc":
+            for device in self.others(axis):
+                pl.semaphore_signal(barrier, inc=1, device_id=device, device_id_type=MESH)
+                count += 1
+        pl.semaphore_wait(barrier, count)
+
+
+class Sends:
+    def __init__(self, send, recv):
+        self.send, self.recv, self.used, self.started = send, recv, 0, []
+
+    def start(self, source, target, device):
+        copy = pltpu.make_async_remote_copy(
+            src_ref=source,
+            dst_ref=target,
+            send_sem=self.send.at[self.used],
+            recv_sem=self.recv.at[self.used],
+            device_id=device,
+            device_id_type=MESH,
+        )
+        self.used += 1
+        copy.start()
+        self.started.append(copy)
+        return copy
+
+    def finish(self):
+        for copy in self.started:
+            copy.wait_send()
+
+
+class Gather:
+    def __init__(self, grid, source, target, order, local, send, recv):
+        self.grid, self.source, self.target, self.order = grid, source, target, order
+        self.local, self.sends, self.current = local, Sends(send, recv), []
+
+    def start(self):
+        z, y, x, core = self.grid.here()
+        mine = self.target.at[z, y, x, core]
+        self.own = pltpu.make_async_copy(self.source, mine, self.local)
+        self.own.start()
+        self.current = [
+            self.sends.start(self.source, mine, device) for device in self.grid.others("z")
+        ]
+
+    def wait(self):
+        for copy in self.current:
+            copy.wait_recv()
+        self.current = []
+
+    def step(self, number):
+        z, y, x, core = self.grid.here()
+        self.wait()
+        if number == 0:
+            self.own.wait()
+            view = self.target.at[:, y, x, core]
+        elif number == 1:
+            view = self.target.at[:, :, x, core] if self.order[0] == "y" else self.target.at[:, y, :, core]
+        else:
+            view = self.target.at[:, :, :, core]
+        axis = (self.order + "c")[number]
+        self.current = [self.sends.start(view, view, device) for device in self.grid.others(axis)]
+
+    def finish(self):
+        self.wait()
+        self.sends.finish()
+
+
+class Reduce:
+    def __init__(self, grid, source, order, held, parts, local, send, recv):
+        self.grid, self.source, self.order, self.held = grid, source, order, held
+        self.parts, self.local, self.sends, self.current = parts, local, Sends(send, recv), []
+
+    def start(self):
+        z, y, x, core = self.grid.here()
+        self.own = pltpu.make_async_copy(self.source.at[:, :, :, core], self.held, self.local)
+        self.own.start()
+        device = self.grid.others("c")[0]
+        self.current = [
+            self.sends.start(self.source.at[:, :, :, 1 - core], self.parts[0].at[0], device)
+        ]
+
+    def take(self, view, parts):
+        for copy in self.current:
+            copy.wait_recv()
+        for i in range(len(self.current)):
+            view[...] += parts[i]
+
+    def step(self, number):
+        z, y, x, core = self.grid.here()
+        held, first = self.held, self.order[0]
+        if number == 0:
+            self.own.wait()
+            view = held
+        elif number == 1:
+            view = held.at[:, y] if first == "y" else held.at[:, :, x]
+        else:
+            view = held.at[:, y, x]
+        self.take(view, self.parts[number])
+        axis = (self.order + "z")[number]
+        devices = self.grid.others(axis)
+        self.current = []
+        for i, device in enumerate(devices):
+            if axis == "z":
+                part = held.at[(z + i + 1) % self.grid.z, y, x]
+            elif axis == "y":
+                other = (y + i + 1) % self.grid.y
+                part = held.at[:, other] if number == 0 else held.at[:, other, x]
+            else:
+                other = (x + i + 1) % self.grid.x
+                part = held.at[:, :, other] if number == 0 else held.at[:, y, other]
+            self.current.append(self.sends.start(part, self.parts[number + 1].at[i], device))
+
+    def result(self):
+        z, y, x, core = self.grid.here()
+        for copy in self.current:
+            copy.wait_recv()
+        total = self.held[z, y, x]
+        for i in range(len(self.current)):
+            total = total + self.parts[3][i]
+        return total
+
+    def finish(self):
+        self.sends.finish()
+
+
+def reduce_scratch(grid, shape, order):
+    z, y, x = grid.z, grid.y, grid.x
+    first = y if order[0] == "y" else x
+    second = x if order[0] == "y" else y
+    return [
+        pltpu.VMEM((z, y, x) + shape, f32),
+        pltpu.VMEM((1, z, y, x) + shape, f32),
+        pltpu.VMEM((first - 1, z, second) + shape, f32),
+        pltpu.VMEM((second - 1, z) + shape, f32),
+        pltpu.VMEM((z - 1,) + shape, f32),
+    ]
+
+
+def vmem_specs(count):
+    return [pl.BlockSpec(memory_space=pltpu.VMEM)] * count
+
+
+def any_specs(count):
+    return [pl.BlockSpec(memory_space=pl.ANY)] * count
+
+
+def sentence_bounds(lengths, marks, first):
+    start = jnp.zeros(marks.shape, jnp.int32)
+    end = jnp.zeros(marks.shape, jnp.int32)
+    at = jnp.int32(0)
+    for e in range(lengths.shape[1]):
+        after = at + lengths[0, e]
+        start = jnp.where(marks == first + e, at, start)
+        end = jnp.where(marks == first + e, after, end)
+        at = after
+    return start, end
+
+
+def in_sentence(positions, start, end):
+    return jnp.logical_and(positions >= start, positions < end).astype(f32)
+
+
+def query_pack(transposed, extra):
+    high, low = split(transposed[: transposed.shape[0] // 2])
+    return cat([high, low, high, extra.astype(bf16)], 0)
+
+
+def key_pack(doubled, extra):
+    lanes = iota(doubled.shape, 1)
+    half = doubled.shape[1] // 2
+    high, low = split_wide(doubled)
+    return cat([high.astype(bf16), jnp.where(lanes < half, low, extra).astype(bf16)], 1)
+
+
+def half_split(doubled, axis):
+    half = doubled.shape[axis] // 2
+    high, low = split_wide(doubled)
+    return jnp.where(iota(doubled.shape, axis) < half, high, low).astype(bf16)
+
+
+def twice(pair):
+    half = pair.shape[1] // 2
+    turned = pltpu.roll(pair, half, 1)
+    lanes = iota(pair.shape, 1)
+    return jnp.where(lanes < half, pair, turned), jnp.where(lanes < half, turned, pair)
+
+
+def pick(wide, route, head):
+    lanes = iota((wide.shape[0], 2 * head), 1) // head
+    total = None
+    for group in range(wide.shape[1] // (2 * head)):
+        part = jnp.where(lanes + 2 * group == route, wide[:, group * 2 * head : (group + 1) * 2 * head], 0.0)
+        total = part if total is None else total + part
+    return total + pltpu.roll(total, head, 1)
+
+
+def spread(doubled, route, experts):
+    head = doubled.shape[1] // 2
+    lanes = iota(doubled.shape, 1) // head
+    return cat([jnp.where(lanes + 2 * group == route, doubled, 0.0) for group in range(experts // 2)], 1)
+
+
+def normalise(values):
+    centre = values - jnp.mean(values, axis=-1, keepdims=True)
+    scale = lax.rsqrt(jnp.mean(centre * centre, axis=-1, keepdims=True) + norm_eps)
+    return centre * scale, scale
+
+
+def norm_back(grad, unit, scale, gain):
+    inner = grad * gain
+    mean = jnp.mean(inner, axis=-1, keepdims=True)
+    along = jnp.mean(inner * unit, axis=-1, keepdims=True)
+    return scale * (inner - mean - unit * along)
+
+
+def forward_kernel(
+    grid, head, experts,
+    lengths, tokens, routes, packed, out_shard, up_shard, down_shard,
+    front_all, vectors, bias, heads_out, queries, logsum, gates, keyval, out_all, up_all, down_all,
+    high_w, low_w, query_t, key_p, value_t, scores, accum, peak, total, extra, even, odd,
+    local, send, recv, kv_send, kv_recv,
+):
+    span, width = tokens.shape
+    z, y, x, core = grid.here()
+    grid.barrier()
+    columns = packed.shape[1]
+    half = columns // 2
+    items = [
+        (packed.at[:, :half], front_all.at[:, :, :, :, :, :half], "yx"),
+        (packed.at[:, half:], front_all.at[:, :, :, :, :, half:], "xy"),
+        (out_shard, out_all, "yx"),
+        (up_shard.at[:, : up_shard.shape[1] // 2], up_all.at[:, :, :, :, :, : up_shard.shape[1] // 2], "yx"),
+        (up_shard.at[:, up_shard.shape[1] // 2 :], up_all.at[:, :, :, :, :, up_shard.shape[1] // 2 :], "xy"),
+        (down_shard.at[: down_shard.shape[0] // 2], down_all.at[:, :, :, :, : down_shard.shape[0] // 2], "yx"),
+        (down_shard.at[down_shard.shape[0] // 2 :], down_all.at[:, :, :, :, down_shard.shape[0] // 2 :], "xy"),
+    ]
+    gathers = [
+        Gather(grid, source, target, order, local.at[i], send.at[i], recv.at[i])
+        for i, (source, target, order) in enumerate(items)
+    ]
+    front, rest = gathers[:2], gathers[2:]
+    for item in front:
+        item.start()
+    for number in range(3):
+        for item in front:
+            item.step(number)
+        if number == 0:
+            for item in rest[:3]:
+                item.start()
+    for item in front:
+        item.wait()
+    for item in rest[3:]:
+        item.start()
+    whole = front_all[...].reshape(width, columns)
+    high_w[...], low_w[...] = split(whole)
+    wide = experts * head
+    tail = whole[:, wide + 2 * head :]
+    extra[...] = tail
+    turned = tail.T
+    vectors[...] = turned[8:16]
+    shard = width // grid.count
+    piece = bias.shape[1] // grid.count
+    per_tile = 128 // piece
+    pieces = extra[pl.ds(0, grid.count, stride=shard), :]
+    even[...] = pltpu.roll(pieces, piece, 1)
+    odd[...] = pieces
+    lanes = iota((1, 128), 1)
+    for q in range(bias.shape[1] // 128):
+        bias[0:1, q * 128 : (q + 1) * 128] = jnp.where(
+            lanes < piece, even[per_tile * q : per_tile * q + 1], odd[per_tile * q + 1 : per_tile * q + 2]
+        )
+    gain, shift = vectors[0:1], vectors[1:2]
+    seq_at = (x * 2 + core) * span
+    block = min(256, span)
+
+    def project(i, carry):
+        rows = rows_at(i, block)
+        normed = normalise(tokens[rows])[0] * gain + shift
+        result = dot_nn(split(normed), (high_w[...], low_w[...]))
+        lane = iota((block, 2 * head), 1)
+        picked_routes = [routes[rows, k : k + 1] for k in range(2)]
+        logits = result[:, wide + 2 * head :]
+        chosen = [
+            jnp.sum(jnp.where(lane == route, logits, 0.0), axis=1, keepdims=True) for route in picked_routes
+        ]
+        top = jnp.maximum(chosen[0], chosen[1])
+        raw = [jnp.exp(c - top) for c in chosen]
+        norm = raw[0] + raw[1]
+        gates[rows] = jnp.where(lane < head, raw[0] / norm, raw[1] / norm)
+        keyval[x, core, rows] = result[:, wide : wide + 2 * head]
+        marks = iota((head, 1), 0)
+        start, end = sentence_bounds(lengths, marks, 0)
+        positions = seq_at + i * block + iota((1, block), 1)
+        inside = in_sentence(positions, start, end)
+        for k in range(2):
+            query = pick(result[:, :wide], picked_routes[k], head) * (log2e * head**-0.5)
+            queries[rows_at(k * (span // block) + i, block)] = query
+            query_t[:, rows_at(k * (span // block) + i, block)] = query_pack(query.T, inside)
+        return carry
+
+    lax.fori_loop(0, span // block, project, 0)
+    moves = Sends(kv_send, kv_recv)
+    mine = keyval.at[x, core]
+    sibling = grid.others("c")[0]
+    to_sibling = moves.start(mine, mine, sibling)
+    across = [moves.start(mine, mine, device) for device in grid.others("x")]
+    for item in rest[:3]:
+        item.step(0)
+
+    accum[...] = jnp.zeros_like(accum)
+    peak[...] = jnp.full_like(peak, -3e38)
+    total[...] = jnp.zeros_like(total)
+    s_tile, t_tile = min(512, span), min(1024, 2 * span)
+    s_count, t_count = span // s_tile, 2 * span // t_tile
+
+    def attend(chunk_x, chunk_core):
+        at = (chunk_x * 2 + chunk_core) * span
+
+        def prepare(i, carry):
+            rows = rows_at(i, block)
+            keys, values = twice(keyval[chunk_x, chunk_core, rows])
+            marks = iota((1, 2 * head), 1)
+            start, end = sentence_bounds(lengths, marks, head)
+            positions = at + i * block + iota((block, 1), 0)
+            outside = jnp.where(marks - head < lengths.shape[1], (in_sentence(positions, start, end) - 1.0) * far, 0.0)
+            key_p[rows] = key_pack(keys, outside)
+            value_t[:, rows] = half_split(values.T, 0)
+            return carry
+
+        lax.fori_loop(0, span // block, prepare, 0)
+
+        def tile(i, carry):
+            s_rows = rows_at(i // t_count, s_tile)
+            t_cols = rows_at(i % t_count, t_tile)
+            scores[...] = dot(key_p[s_rows], query_t[:, t_cols])
+            old = peak[0:1, t_cols]
+            new = jnp.maximum(old, jnp.max(scores[...], axis=0, keepdims=True))
+            fade = jnp.exp2(old - new)
+            probs = jnp.exp2(scores[...] - new)
+            high, low = split(probs)
+            weights = value_t[:, s_rows]
+            add = dot(cat([weights, weights], 1), cat([high, low], 0))
+            total[0:1, t_cols] = total[0:1, t_cols] * fade + jnp.sum(probs, axis=0, keepdims=True)
+            accum[:, t_cols] = accum[:, t_cols] * fade + add
+            peak[0:1, t_cols] = new
+            return carry
+
+        lax.fori_loop(0, s_count * t_count, tile, 0)
+
+    attend(x, core)
+    to_sibling.wait_recv()
+    for item in rest[:3]:
+        item.step(1)
+    forwards = []
+    attend(x, 1 - core)
+    for i in range(1, grid.x):
+        across[i - 1].wait_recv()
+        view = keyval.at[(x - i + grid.x) % grid.x, core]
+        forward = moves.start(view, view, sibling)
+        if i == 1:
+            for item in rest[3:]:
+                item.step(0)
+        attend((x - i + grid.x) % grid.x, core)
+        forward.wait_recv()
+        if i == 1:
+            for item in rest[:3]:
+                item.step(2)
+            for item in rest[3:]:
+                item.step(1)
+        attend((x - i + grid.x) % grid.x, 1 - core)
+    for item in rest[3:]:
+        item.step(2)
+
+    def finish(i, carry):
+        cols = rows_at(i, block)
+        norm = total[0:1, cols]
+        result = (accum[:head, cols] + accum[head:, cols]) / norm
+        heads_out[cols] = cat([result, result], 0).T
+        logsum[0:1, cols] = peak[0:1, cols] + jnp.log2(norm)
+        return carry
+
+    lax.fori_loop(0, 2 * span // block, finish, 0)
+    for item in gathers:
+        item.finish()
+    moves.finish()
+
+
+def forward(grid, experts, head, lengths, tokens, routes, packed, out_shard, up_shard, down_shard):
+    span, width = tokens.shape
+    columns = packed.shape[1]
+    ff = up_shard.shape[1]
+    lead = grid.lead
+    shapes = [
+        lead + packed.shape,
+        (8, width),
+        (1, ff),
+        (2 * span, 2 * head),
+        (2 * span, 2 * head),
+        (1, 2 * span),
+        (span, 2 * head),
+        (grid.x, 2, span, 2 * head),
+        lead + out_shard.shape,
+        lead + up_shard.shape,
+        lead + down_shard.shape,
+    ]
+    items = 7
+    return pl.pallas_call(
+        functools.partial(forward_kernel, grid, head, experts),
+        out_shape=[jax.ShapeDtypeStruct(shape, f32) for shape in shapes],
+        in_specs=[pl.BlockSpec(memory_space=pltpu.SMEM)] + vmem_specs(3) + any_specs(3),
+        out_specs=vmem_specs(8) + any_specs(3),
+        scratch_shapes=[
+            pltpu.VMEM((width, columns), bf16),
+            pltpu.VMEM((width, columns), bf16),
+            pltpu.VMEM((4 * head, 2 * span), bf16),
+            pltpu.VMEM((span, 4 * head), bf16),
+            pltpu.VMEM((2 * head, span), bf16),
+            pltpu.VMEM((min(512, span), min(1024, 2 * span)), f32),
+            pltpu.VMEM((2 * head, 2 * span), f32),
+            pltpu.VMEM((1, 2 * span), f32),
+            pltpu.VMEM((1, 2 * span), f32),
+            pltpu.VMEM((width, 128), f32),
+            pltpu.VMEM((grid.count, 128), f32),
+            pltpu.VMEM((grid.count, 128), f32),
+            pltpu.SemaphoreType.DMA((items,)),
+            pltpu.SemaphoreType.DMA((items, grid.copies())),
+            pltpu.SemaphoreType.DMA((items, grid.copies())),
+            pltpu.SemaphoreType.DMA((2 * grid.x - 1,)),
+            pltpu.SemaphoreType.DMA((2 * grid.x - 1,)),
+        ],
+        compiler_params=pltpu.CompilerParams(
+            collective_id=0, has_side_effects=True, vmem_limit_bytes=vmem_limit
+        ),
+        name="front_and_attention",
+    )(lengths, tokens, routes, packed, out_shard, up_shard, down_shard)
+
+
+def middle_kernel(
+    head, experts,
+    tokens, cotangent, heads, gates, routes, vectors, bias, out_w, up_w, down_w,
+    output, middle_grad, up_grad, down_grad, out_grad, vector_grad, bias_grad, heads_grad, chosen_grad,
+    out_h, out_l, up_h, up_l, down_h, down_l, norm_h, norm_l, cot_h, cot_l, unit, scale_ref, norm_grad,
+):
+    span, width = tokens.shape
+    ff = up_w.shape[1]
+    block, part = min(512, span), 512
+    out_h[...], out_l[...] = split(out_w[...])
+
+    def halve(i, carry):
+        rows = rows_at(i, width // 4)
+        up_h[rows], up_l[rows] = split(up_w[rows])
+        rows = rows_at(i, ff // 4)
+        down_h[rows], down_l[rows] = split(down_w[rows])
+        return carry
+
+    lax.fori_loop(0, 4, halve, 0)
+    up_grad[...] = jnp.zeros_like(up_grad)
+    down_grad[...] = jnp.zeros_like(down_grad)
+    out_grad[...] = jnp.zeros_like(out_grad)
+    vector_grad[...] = jnp.zeros_like(vector_grad)
+    bias_grad[...] = jnp.zeros_like(bias_grad)
+    gain, shift, last = vectors[2:3], vectors[3:4], vectors[4:5]
+
+    def tokens_block(i, carry):
+        rows = rows_at(i, block)
+        second = rows_at(span // block + i, block)
+        gate = gates[rows]
+        turned = pltpu.roll(gate, head, 1)
+        lane = iota(gate.shape, 1)
+        gate_k = [jnp.where(lane < head, gate, turned), jnp.where(lane < head, turned, gate)]
+        route = [routes[rows, k : k + 1] for k in range(2)]
+        own = [heads[rows], heads[second]]
+        mixed = sum(spread(gate_k[k] * own[k], route[k], experts) for k in range(2))
+        mixed_s = split(mixed)
+        middle = tokens[rows] + dot_nn(mixed_s, (out_h[...], out_l[...]))
+        unit_v, scale = normalise(middle)
+        unit[...] = unit_v
+        scale_ref[...] = jnp.broadcast_to(scale, scale_ref.shape)
+        norm_h[...], norm_l[...] = split(unit_v * gain + shift)
+        cot = cotangent[rows]
+        cot_h[...], cot_l[...] = split(cot)
+        output[rows] = middle + last
+        norm_grad[...] = jnp.zeros_like(norm_grad)
+
+        def hidden_part(j, carry):
+            cols = rows_at(j, part)
+            cot_s = (cot_h[...], cot_l[...])
+            norm_s = (norm_h[...], norm_l[...])
+            up_s = (up_h[:, cols], up_l[:, cols])
+            down_s = (down_h[cols], down_l[cols])
+            pre = dot_nn(norm_s, up_s) + bias[0:1, cols]
+            back = dot_nt(cot_s, down_s)
+            square = pre * pre
+            wave = jnp.tanh(math.sqrt(2.0 / math.pi) * (pre + 0.044715 * (square * pre)))
+            half = 0.5 * (1.0 + wave)
+            hidden_s = split(pre * half)
+            slope = half + (0.5 * math.sqrt(2.0 / math.pi)) * pre * (1.0 - wave * wave) * (
+                1.0 + (3.0 * 0.044715) * square
+            )
+            pre_grad = back * slope
+            pre_s = split(pre_grad)
+            output[rows] += dot_nn(hidden_s, down_s)
+            norm_grad[...] += dot_nt(pre_s, up_s)
+            down_grad[cols] += dot_tn(hidden_s, cot_s)
+            up_grad[:, cols] += dot_tn(norm_s, pre_s)
+            bias_grad[0:1, cols] += jnp.sum(pre_grad, axis=0, keepdims=True)
+            return carry
+
+        lax.fori_loop(0, ff // part, hidden_part, 0)
+        grad = norm_grad[...]
+        unit_v = unit[...]
+        vector_grad[2:3] += jnp.sum(grad * unit_v, axis=0, keepdims=True)
+        vector_grad[3:4] += jnp.sum(grad, axis=0, keepdims=True)
+        vector_grad[4:5] += jnp.sum(cot, axis=0, keepdims=True)
+        mid = cot + norm_back(grad, unit_v, scale_ref[:, 0:1], gain)
+        middle_grad[rows] = mid
+        mid_s = split(mid)
+        out_grad[...] += dot_tn(mixed_s, mid_s)
+        grad_mixed = dot_nt(mid_s, (out_h[...], out_l[...]))
+        gates_grad = []
+        for k in range(2):
+            picked = pick(grad_mixed, route[k], head)
+            gate_grad = jnp.sum(jnp.where(lane < head, picked * own[k], 0.0), axis=1, keepdims=True)
+            gates_grad.append(gate_grad)
+            delta = gate_grad * gate_k[k]
+            heads_grad[rows_at(k * (span // block) + i, block)] = jnp.where(
+                lane < head, gate_k[k] * picked, jnp.where(lane == head, delta, 0.0)
+            )
+        both = gate_k[0] * gates_grad[0] + gate_k[1] * gates_grad[1]
+        chosen_grad[rows] = jnp.where(
+            lane == 0, gate_k[0] * (gates_grad[0] - both), gate_k[1] * (gates_grad[1] - both)
+        )
+        return carry
+
+    lax.fori_loop(0, span // block, tokens_block, 0)
+
+
+def middle(experts, head, tokens, cotangent, heads, gates, routes, vectors, bias, out_w, up_w, down_w):
+    span, width = tokens.shape
+    ff = up_w.shape[1]
+    block = min(512, span)
+    shapes = [
+        (span, width),
+        (span, width),
+        (width, ff),
+        (ff, width),
+        (experts * head, width),
+        (8, width),
+        (1, ff),
+        (2 * span, 2 * head),
+        (span, 2 * head),
+    ]
+    return pl.pallas_call(
+        functools.partial(middle_kernel, head, experts),
+        out_shape=[jax.ShapeDtypeStruct(shape, f32) for shape in shapes],
+        in_specs=vmem_specs(10),
+        out_specs=vmem_specs(9),
+        scratch_shapes=[
+            pltpu.VMEM(out_w.shape, bf16),
+            pltpu.VMEM(out_w.shape, bf16),
+            pltpu.VMEM(up_w.shape, bf16),
+            pltpu.VMEM(up_w.shape, bf16),
+            pltpu.VMEM(down_w.shape, bf16),
+            pltpu.VMEM(down_w.shape, bf16),
+            pltpu.VMEM((block, width), bf16),
+            pltpu.VMEM((block, width), bf16),
+            pltpu.VMEM((block, width), bf16),
+            pltpu.VMEM((block, width), bf16),
+            pltpu.VMEM((block, width), f32),
+            pltpu.VMEM((block, 128), f32),
+            pltpu.VMEM((block, width), f32),
+        ],
+        compiler_params=pltpu.CompilerParams(vmem_limit_bytes=vmem_limit),
+        name="feed_forward",
+    )(tokens, cotangent, heads, gates, routes, vectors, bias, out_w, up_w, down_w)
+
+
+def backward_kernel(
+    grid, head, experts,
+    lengths, tokens, middle_grad, routes, front_all, keyval, queries, logsum, heads_grad, chosen_grad,
+    vectors, vector_grad, bias_grad, up_grad, down_grad, out_grad,
+    input_grad, front_sum, up_sum, down_sum, out_sum,
+    query_t, query_n, grad_t, grad_n, key_p, value_p, key_t, query_grad, tile_k, tile_v,
+    chunk_grad, chunk_in, cross_in, front_grad, high_w, low_w, extra, even, *rest,
+):
+    reduces, sems = rest[:25], rest[25:]
+    local, send, recv, kv_send, kv_recv = sems
+    span, width = tokens.shape
+    z, y, x, core = grid.here()
+    grid.barrier()
+    columns = front_all.shape[-1]
+    half = columns // 2
+    wide = experts * head
+    sources = [
+        (up_grad, "yx"),
+        (down_grad, "xy"),
+        (out_grad, "yx"),
+        (front_grad.at[:, :, :, :, :, :half], "yx"),
+        (front_grad.at[:, :, :, :, :, half:], "xy"),
+    ]
+    items = [
+        Reduce(grid, source, order, reduces[5 * i], reduces[5 * i + 1 : 5 * i + 5], local.at[i], send.at[i], recv.at[i])
+        for i, (source, order) in enumerate(sources)
+    ]
+    early, late = items[:3], items[3:]
+    for item in early:
+        item.start()
+    block = min(256, span)
+    blocks = span // block
+    seq_at = (x * 2 + core) * span
+
+    def prepare_queries(i, carry):
+        rows = rows_at(i, block)
+        marks = iota((head, 1), 0)
+        start, end = sentence_bounds(lengths, marks, 0)
+        positions = seq_at + (i % blocks) * block + iota((1, block), 1)
+        rest_ls = -logsum[0:1, rows]
+        one = rest_ls.astype(bf16).astype(f32)
+        two = (rest_ls - one).astype(bf16).astype(f32)
+        three = rest_ls - one - two
+        inside = in_sentence(positions, start, end)
+        inside = jnp.where(marks == 8, one, jnp.where(marks == 9, two, jnp.where(marks == 10, three, inside)))
+        query = queries[rows]
+        query_t[:, rows] = query_pack(query.T, inside)
+        query_n[rows] = half_split(query, 1)
+        grad = heads_grad[rows]
+        turned = grad.T
+        rest_d = -turned[head : head + 1]
+        one = rest_d.astype(bf16).astype(f32)
+        two = (rest_d - one).astype(bf16).astype(f32)
+        three = rest_d - one - two
+        terms = jnp.where(marks == 0, one, jnp.where(marks == 1, two, jnp.where(marks == 2, three, 0.0)))
+        grad_t[:, rows] = query_pack(turned, terms)
+        grad_n[rows] = half_split(twice(grad)[0], 1)
+        return carry
+
+    lax.fori_loop(0, 2 * blocks, prepare_queries, 0)
+    query_grad[...] = jnp.zeros_like(query_grad)
+    s_tile, t_tile = min(512, span), min(512, span)
+    t_count = 2 * span // t_tile
+
+    def chunk(chunk_x, chunk_core, target):
+        at = (chunk_x * 2 + chunk_core) * span
+
+        def prepare(i, carry):
+            rows = rows_at(i, block)
+            keys, values = twice(keyval[chunk_x, chunk_core, rows])
+            marks = iota((1, 2 * head), 1)
+            start, end = sentence_bounds(lengths, marks, head)
+            positions = at + i * block + iota((block, 1), 0)
+            outside = jnp.where(marks - head < lengths.shape[1], (in_sentence(positions, start, end) - 1.0) * far, 0.0)
+            ones = jnp.logical_and(marks - head >= 8, marks - head < 11)
+            key_p[rows] = key_pack(keys, jnp.where(ones, 1.0, outside))
+            few = jnp.logical_and(marks - head >= 0, marks - head < 3).astype(f32)
+            value_p[rows] = key_pack(values, jnp.broadcast_to(few, values.shape))
+            key_t[:, rows] = half_split(keys.T, 0)
+            return carry
+
+        lax.fori_loop(0, blocks, prepare, 0)
+
+        def key_rows(i, carry):
+            s_rows = rows_at(i, s_tile)
+            tile_k[...] = jnp.zeros_like(tile_k)
+            tile_v[...] = jnp.zeros_like(tile_v)
+
+            def tile(j, carry):
+                t_cols = rows_at(j, t_tile)
+                probs = jnp.exp2(dot(key_p[s_rows], query_t[:, t_cols]))
+                probs_h, probs_l = split(probs)
+                grads = probs * dot(value_p[s_rows], grad_t[:, t_cols])
+                grads_h, grads_l = split(grads)
+                grad_rows, query_rows = grad_n[t_cols], query_n[t_cols]
+                tile_v[...] += dot(cat([probs_h, probs_l], 1), cat([grad_rows, grad_rows], 0))
+                tile_k[...] += dot(cat([grads_h, grads_l], 1), cat([query_rows, query_rows], 0))
+                keys = key_t[:, s_rows]
+                query_grad[:, t_cols] += dot(cat([keys, keys], 1), cat([grads_h, grads_l], 0))
+                return carry
+
+            lax.fori_loop(0, t_count, tile, 0)
+            lane = iota((s_tile, 2 * head), 1)
+            k_part, v_part = tile_k[...], tile_v[...]
+            target[s_rows] = jnp.where(
+                lane < head,
+                (k_part + pltpu.roll(k_part, head, 1)) * (1.0 / log2e),
+                v_part + pltpu.roll(v_part, head, 1),
+            )
+            return carry
+
+        lax.fori_loop(0, span // s_tile, key_rows, 0)
+
+    moves = Sends(kv_send, kv_recv)
+    sibling = grid.others("c")[0]
+    step = 0
+    crossing = []
+    for i in range(1, grid.x):
+        there = (x + i) % grid.x
+        chunk(there, 1 - core, chunk_grad.at[2 * i])
+        over = moves.start(chunk_grad.at[2 * i], chunk_in.at[i], sibling)
+        if i == 1:
+            for item in early:
+                item.step(0)
+        chunk(there, core, chunk_grad.at[2 * i + 1])
+        over.wait_recv()
+        chunk_grad[2 * i + 1] += chunk_in[i]
+        crossing.append(moves.start(chunk_grad.at[2 * i + 1], cross_in.at[i - 1], grid.others("x")[i - 1]))
+    for item in early:
+        item.step(1)
+    chunk(x, 1 - core, chunk_grad.at[0])
+    over = moves.start(chunk_grad.at[0], chunk_in.at[0], sibling)
+    for item in early:
+        item.step(2)
+    chunk(x, core, chunk_grad.at[1])
+    over.wait_recv()
+    for copy in crossing:
+        copy.wait_recv()
+    own = chunk_grad.at[1]
+    own[...] += chunk_in[0]
+    for i in range(1, grid.x):
+        own[...] += cross_in[i - 1]
+
+    whole = front_all[...].reshape(width, columns)
+    high_w[...], low_w[...] = split(whole)
+    front_rows = front_grad.reshape(width, columns)
+    front_rows[...] = jnp.zeros_like(front_rows)
+    gain, shift = vectors[0:1], vectors[1:2]
+
+    def project_back(i, carry):
+        rows = rows_at(i, block)
+        unit, scale = normalise(tokens[rows])
+        normed_s = split(unit * gain + shift)
+        parts = []
+        lane = iota((block, 2 * head), 1)
+        logits = jnp.zeros((block, 2 * head), f32)
+        for k in range(2):
+            cols = rows_at(k * blocks + i, block)
+            grad = (query_grad[:head, cols] + query_grad[head:, cols]) * (head**-0.5)
+            grad = cat([grad, grad], 0).T
+            parts.append(spread(grad, routes[rows, k : k + 1], experts))
+            logits = logits + jnp.where(lane == routes[rows, k : k + 1], chosen_grad[rows, k : k + 1], 0.0)
+        all_s = split(cat([parts[0] + parts[1], own[rows], logits], 1))
+        front_rows[...] += dot_tn(normed_s, all_s)
+        grad = dot_nt(all_s, (high_w[...], low_w[...]))
+        extra[0:1] += jnp.sum(grad * unit, axis=0, keepdims=True)
+        extra[1:2] += jnp.sum(grad, axis=0, keepdims=True)
+        input_grad[rows] = middle_grad[rows] + norm_back(grad, unit, scale, gain)
+        return carry
+
+    extra[...] = jnp.zeros_like(extra)
+    extra[0:8] = vector_grad[...]
+    lax.fori_loop(0, blocks, project_back, 0)
+    shard = width // grid.count
+    piece = bias_grad.shape[1] // grid.count
+    per_tile = 128 // piece
+    lanes = iota((1, 128), 1)
+    for q in range(bias_grad.shape[1] // 128):
+        both = bias_grad[0:1, q * 128 : (q + 1) * 128]
+        even[per_tile * q : per_tile * q + 1] = jnp.where(lanes < piece, 0.0, pltpu.roll(both, piece, 1))
+        even[per_tile * q + 1 : per_tile * q + 2] = jnp.where(lanes < piece, 0.0, both)
+    lane = iota((width, 128), 1)
+    columns_of = cat([jnp.zeros((8, width), f32), extra[0:8], jnp.zeros((112, width), f32)], 0).T
+    place = (iota((width, grid.count), 0) == iota((width, grid.count), 1) * shard).astype(bf16)
+    bias_h, bias_l = split(even[...])
+    bias_m = (even[...] - bias_h.astype(f32) - bias_l.astype(f32)).astype(bf16)
+    spread_bias = dot(cat([place, place, place], 1), cat([bias_h, bias_l, bias_m], 0))
+    front_rows[:, wide + 2 * head :] += columns_of + spread_bias
+    for item in late:
+        item.start()
+    up_sum[...] = early[0].result()
+    down_sum[...] = early[1].result()
+    out_sum[...] = early[2].result()
+    for number in range(3):
+        for item in late:
+            item.step(number)
+    front_sum[:, :half] = late[0].result()
+    front_sum[:, half:] = late[1].result()
+    for item in items:
+        item.finish()
+    moves.finish()
+
+
+def backward(
+    grid, experts, head, lengths, tokens, middle_grad, routes, front_all, keyval, queries, logsum, heads_grad,
+    chosen_grad, vectors, vector_grad, bias_grad, up_grad, down_grad, out_grad,
+):
+    span, width = tokens.shape
+    ff = up_grad.shape[1]
+    columns = front_all.shape[-1]
+    shard, ff_shard = width // grid.count, ff // grid.count
+    lead = grid.lead
+    up_grad = up_grad.reshape(lead + (shard, ff))
+    down_grad = down_grad.reshape(lead + (ff_shard, width))
+    out_grad = out_grad.reshape(lead + (out_grad.shape[0] // grid.count, width))
+    out_shapes = [(span, width), (shard, columns), (shard, ff), (ff_shard, width), out_grad.shape[4:]]
+    tile = min(512, span)
+    reduce_shapes = [
+        ((shard, ff), "yx"),
+        ((ff_shard, width), "xy"),
+        (out_grad.shape[4:], "yx"),
+        ((shard, columns // 2), "yx"),
+        ((shard, columns // 2), "xy"),
+    ]
+    items = len(reduce_shapes)
+    scratch = [
+        pltpu.VMEM((4 * head, 2 * span), bf16),
+        pltpu.VMEM((2 * span, 2 * head), bf16),
+        pltpu.VMEM((4 * head, 2 * span), bf16),
+        pltpu.VMEM((2 * span, 2 * head), bf16),
+        pltpu.VMEM((span, 4 * head), bf16),
+        pltpu.VMEM((span, 4 * head), bf16),
+        pltpu.VMEM((2 * head, span), bf16),
+        pltpu.VMEM((2 * head, 2 * span), f32),
+        pltpu.VMEM((tile, 2 * head), f32),
+        pltpu.VMEM((tile, 2 * head), f32),
+        pltpu.VMEM((2 * grid.x, span, 2 * head), f32),
+        pltpu.VMEM((grid.x, span, 2 * head), f32),
+        pltpu.VMEM((grid.x - 1, span, 2 * head), f32),
+        pltpu.VMEM(lead + (shard, columns), f32),
+        pltpu.VMEM((width, columns), bf16),
+        pltpu.VMEM((width, columns), bf16),
+        pltpu.VMEM((8, width), f32),
+        pltpu.VMEM((grid.count, 128), f32),
+    ]
+    for shape, order in reduce_shapes:
+        scratch += reduce_scratch(grid, tuple(shape), order)
+    scratch += [
+        pltpu.SemaphoreType.DMA((items,)),
+        pltpu.SemaphoreType.DMA((items, grid.copies() + 1)),
+        pltpu.SemaphoreType.DMA((items, grid.copies() + 1)),
+        pltpu.SemaphoreType.DMA((2 * grid.x - 1,)),
+        pltpu.SemaphoreType.DMA((2 * grid.x - 1,)),
+    ]
+    return pl.pallas_call(
+        functools.partial(backward_kernel, grid, head, experts),
+        out_shape=[jax.ShapeDtypeStruct(shape, f32) for shape in out_shapes],
+        in_specs=[pl.BlockSpec(memory_space=pltpu.SMEM)] + vmem_specs(12) + any_specs(3),
+        out_specs=vmem_specs(5),
+        scratch_shapes=scratch,
+        compiler_params=pltpu.CompilerParams(
+            collective_id=1, has_side_effects=True, vmem_limit_bytes=vmem_limit
+        ),
+        name="attention_back",
+    )(
+        lengths, tokens, middle_grad, routes, front_all, keyval, queries, logsum, heads_grad, chosen_grad,
+        vectors, vector_grad, bias_grad, up_grad, down_grad, out_grad,
+    )
+
+
+def update_kernel(factor, head, *refs):
+    front, up, down, out = refs[:4]
+    weights, moments, averages = refs[4:12], refs[12:20], refs[20:28]
+    new_weights, new_moments, new_averages = refs[28:36], refs[36:44], refs[44:52]
+    wide = out.shape[1]
+    tail = front[:, wide + 2 * head :]
+    experts = weights[0].shape[1]
+    vector_rows = weights[7].shape
+    square = cat([tail, jnp.zeros((128 - tail.shape[0], 128), f32)], 0).T
+    piece = weights[5].shape[1]
+    gradients = [
+        tail[:, :experts],
+        front[:, :wide],
+        out[...],
+        front[:, wide : wide + 2 * head],
+        up[...],
+        pltpu.roll(tail[0:8], piece, 1)[0:1, :piece],
+        down[...],
+        square[8 : 8 + vector_rows[0], : vector_rows[1]],
+    ]
+    for i, gradient in enumerate(gradients):
+        scaled = gradient * factor
+        moment = moment_decay * moments[i][...] + scaled
+        weight = weights[i][...] - step_rate * (scaled + moment_decay * moment)
+        new_moments[i][...] = moment
+        new_weights[i][...] = weight
+        new_averages[i][...] = average_decay * averages[i][...] + (1.0 - average_decay) * weight
+
+
+def update_all(factor, head, front, up, down, out, weights, moments, averages):
+    flat = lambda arrays: [a.reshape(1, -1) if a.ndim == 1 else a for a in arrays]
+    shapes = [a.shape for a in weights]
+    weights, moments, averages = flat(weights), flat(moments), flat(averages)
+    results = pl.pallas_call(
+        functools.partial(update_kernel, factor, head),
+        out_shape=[jax.ShapeDtypeStruct(a.shape, f32) for a in weights] * 3,
+        in_specs=vmem_specs(28),
+        out_specs=vmem_specs(24),
+        compiler_params=pltpu.CompilerParams(vmem_limit_bytes=vmem_limit),
+        name="update",
+    )(front, up, down, out, *weights, *moments, *averages)
+    return tuple(r.reshape(shapes[i % 8]) for i, r in enumerate(results))
+
+
+def fused_step(grid, tokens, cotangent, lengths, routes, *params):
+    weights, moments, averages = params[:8], params[8:16], params[16:24]
+    router_weight, query_weight, out_weight, kv_weight, up_weight, up_bias, down_weight, vectors = weights
+    shard, experts = router_weight.shape
+    head = kv_weight.shape[1] // 2
+    piece = up_bias.shape[0]
+    middle_pad = jnp.zeros((shard, 128 - piece - experts - vectors.shape[0]), f32)
+    bias_rows = jnp.concatenate([up_bias[None], jnp.zeros((shard - 1, piece), f32)], axis=0)
+    packed = jnp.concatenate([query_weight, kv_weight, router_weight, vectors.T, middle_pad, bias_rows], axis=1)
+    tokens_in, cotangent_in, routes_in = tokens[0], cotangent[0], routes[0]
+    (
+        front_all, full_vectors, full_bias, heads, queries, logsum, gates, keyval, out_all, up_all, down_all
+    ) = forward(grid, experts, head, lengths, tokens_in, routes_in, packed, out_weight, up_weight, down_weight)
+    full = lambda a: a.reshape(-1, a.shape[-1])
+    (
+        output, middle_grad, up_grad, down_grad, out_grad, vector_grad, bias_grad, heads_grad, chosen_grad
+    ) = middle(
+        experts, head, tokens_in, cotangent_in, heads, gates, routes_in, full_vectors, full_bias,
+        full(out_all), full(up_all), full(down_all),
+    )
+    input_grad, front_sum, up_sum, down_sum, out_sum = backward(
+        grid, experts, head, lengths, tokens_in, middle_grad, routes_in, front_all, keyval, queries, logsum,
+        heads_grad, chosen_grad, full_vectors, vector_grad, bias_grad, up_grad, down_grad, out_grad,
+    )
+    factor = 1.0 / math.sqrt(tokens.shape[0] * tokens.shape[1] * grid.count)
+    updated = update_all(factor, head, front_sum, up_sum, down_sum, out_sum, weights, moments, averages)
+    return (output[None], input_grad[None]) + updated
+
+
+def step_for(mesh):
+    grid = Grid(mesh)
+
+    def step(*args):
+        shard, span = args[4].shape[0], args[0].shape[1]
+        if shard % 8 == 0 and span % 256 == 0 and grid.x > 1 and args[9].shape[0] == 64:
+            return fused_step(grid, *args)
+        return general_step(*args)
+
+    return step
+
+
 def solution(mesh):
     in_specs = (
         P("dp", "seq", None),
@@ -320,5 +1336,5 @@
         P(None, ("dp", "seq")),
     )
     return jax.shard_map(
-        on_device, mesh=mesh, in_specs=in_specs, out_specs=out_specs, check_vma=False
-    )
+        step_for(mesh), mesh=mesh, in_specs=in_specs, out_specs=out_specs, check_vma=False
+    )

time: 881 us -> 280 us (0.32)
  matrix products: 457 us -> 0 us
  Pallas kernels: 0 us -> 265 us
  blocking collectives: 200 us -> 0 us
  waiting for transfers between devices: 113 us -> 0 us
  other arithmetic: 46.9 us -> 0 us
  local copies, waits for them, and re-layouts: 43.5 us -> 13.9 us
  between operations: 15.4 us -> 0.72 us
    dot_general x31 -> x0, matrix products: 457 us -> none  [the longest x18 166 us: matmul(): jnp.dot(left, right, precision=highest, preferred_element_type=jnp.float32)]
    pallas_call x0 -> x4, Pallas kernels: none -> 265 us  [the longest x1 109 us: backward(): pl.pallas_call(functools.partial(backward_kernel, grid, head, experts), o...]
    all_gather x3 -> x0, blocking collectives: 120 us -> none  [the longest x1 43.6 us: on_device(): lax.all_gather(vectors, ('dp', 'seq'), axis=1, tiled=True)]
    psum x1 -> x0, waiting for transfers between devices: 110 us -> none  [on_device(): lax.psum((router_grad, query_weight_grad, out_grad, kv_grad, up_grad, bia...]
    psum x1 -> x0, blocking collectives: 42.6 us -> none  [on_device(): lax.psum((router_grad, query_weight_grad, out_grad, kv_grad, up_grad, bia...]
    unnamed x1 -> x0, blocking collectives: 37.2 us -> none
    reduce_sum x12 -> x0, other arithmetic: 25.9 us -> none  [the longest x1 15.6 us: on_device(): total = jnp.sum(weights_soft, axis=-1)]
    dot_general x7 -> x0, local copies, waits for them, and re-layouts: 19.1 us -> none  [the longest x2 6.97 us: matmul(): jnp.dot(left, right, precision=highest, preferred_element_type=jnp.float32)]
  transfers between devices with their start and end apart: 7 -> 0, of which waited for: 1 -> 0; matrix products, arithmetic and copies ran while one was open for 41% -> 0% of each run, Pallas kernels for 0% -> 0%
where the time goes in v1:
time: 280 us; the launch traced here: 279 us
  Pallas kernels  265 us (95%)
  local copies, waits for them, and re-layouts  13.9 us (5%)
    pallas_call x1, Pallas kernels, backward(): pl.pallas_call(functools.partial(backward_kernel, grid, head, experts), o...  109 us
    pallas_call x1, Pallas kernels, forward(): pl.pallas_call(functools.partial(forward_kernel, grid, head, experts), ou...  88.9 us
    pallas_call x1, Pallas kernels, middle(): pl.pallas_call(functools.partial(middle_kernel, head, experts), out_shape...  64.1 us
    unnamed x15, local copies, waits for them, and re-layouts  11.8 us

profile of v1, /device:TPU:0, one launch (start us, length us, event | category | flops | bytes accessed | tf_op | source)
XLA Modules:
  0.0 279.5 jit_solution(4981252114328543196)
XLA Ops:
  0.7 1.8 copy.54
  2.4 0.7 concatenate.6
  3.1 0.8 copy.56.refs_4_
  3.8 0.0 copy-start
  3.8 0.8 copy.55
  4.6 1.5 concatenate.7.packed
  6.1 88.9 %front_and_attention.1 = (f32[4,2,2,2,16,768]{5,4,3,2,1,0:T(8,128)}, f32[8,512]{1,0:T(8,128)}, f32[1,2048]{1,0:T(1,128)}, f32[2048,128]{1,0:T(8,128)}, f32[2048,...) custom-call(s32[1,6]{1,0:T(1,128)} %lengths.3, ...), custom_call_target="tpu_custom_call" | custom-call | tf_op jit(solution)/shard_map/front_and_attention/pallas_call | solution.py:753
  95.0 64.1 %feed_forward.1 = (f32[1024,512]{1,0:T(8,128)}, f32[1024,512]{1,0:T(8,128)}, f32[512,2048]{1,0:T(8,128)}, f32[2048,512]{1,0:T(8,128)}, f32[512,512]{1,0:T(8,128)...) custom-call(f32[1024,512]{1,0:T(8,128)} %bitcast.19, ...), custom_call_target="tpu_custom_call" | custom-call | tf_op jit(solution)/shard_map/feed_forward/pallas_call | solution.py:899
  159.1 0.0 copy-done
  159.1 0.0 copy-start.1
  159.2 0.0 copy-start.2
  159.2 109.3 %attention_back.1 = (f32[1024,512]{1,0:T(8,128)}, f32[16,768]{1,0:T(8,128)}, f32[16,2048]{1,0:T(8,128)}, f32[64,512]{1,0:T(8,128)}, f32[16,512]{1,0:T(8,128)}) custom-call(s32[1,6]{1,0:T(1,128)} %lengths.3, f32[1024,512]{1,0:T(8,128)} %bitcast.20, f32[1024,512]{1,0:T(8,128)} %get-tuple-element.83.middle_grad, s32[1024,2]{1,0:T(8,128)} %bitcast.23, ...), custom_call_target="tpu_custom_call" | custom-call | tf_op jit(solution)/shard_map/attention_back/pallas_call | solution.py:1178
  268.5 0.0 copy-done.1
  268.5 0.7 copy.58.refs_12_
  269.1 0.0 copy-done.2
  269.2 0.7 copy.59.refs_20_
  269.8 2.5 update.1
  272.3 1.4 copy.60
  273.7 1.4 copy.61
  275.0 1.4 copy.62
  276.4 3.1 %copy.64 = f32[1,1024,512]{2,1,0:T(8,128)} copy(f32[1,1024,512]{2,1,0:T(8,128)} %bitcast.29) | data formatting | bytes 4194304
  (1 shorter events, 0.0 us)
Async XLA Ops:
  3.8 155.3 %copy-start = (f32[16,8]{1,0:T(8,128)}, f32[16,8]{1,0:T(8,128)S(1)}, u32[]{:S(2)}) copy-start(f32[16,8]{1,0:T(8,128)S(1)} %copy.56.refs_4_) | copy-start | bytes 1540
  159.1 109.3 %copy-start.1 = (f32[16,8]{0,1:T(8,128)S(1)}, f32[16,8]{0,1:T(8,128)}, u32[]{:S(2)}) copy-start(f32[16,8]{0,1:T(8,128)} %param.40) | copy-start | bytes 1540
  159.2 110.0 %copy-start.2 = (f32[16,8]{0,1:T(8,128)S(1)}, f32[16,8]{0,1:T(8,128)}, u32[]{:S(2)}) copy-start(f32[16,8]{0,1:T(8,128)} %param.48) | copy-start | bytes 1540
